TPU v7x, 32 devices: a whole 2x2x4 slice. The times are simulated.
32 devices in a mesh: shard: 8 (over y, x, core), rep: 4 (over z).
Axes of the slice: x: 2, y: 2, z: 4, core: 2. Of those that a mesh axis runs over, the one named last changes fastest.
Arguments:
- tokens: bfloat16 [6304, 768], P(('shard', 'rep')), may hold values from -6 to 6
- cotangent: bfloat16 [6304, 768], P(('shard', 'rep')), may hold values from -6 to 6
- expert_index: int32 [6304, 2], P(('shard', 'rep')), may hold values from 0 to 2, as said below
- slot_index: int32 [6304, 2], P(('shard', 'rep')), may hold values from 0 to 111, as said below
- kept_mask: int32 [6304, 2], P(('shard', 'rep')), may hold values from 0 to 1, as said below
- gain_attn: float32 [768], P('shard'), may hold values from 0.5 to 1.5
- shift_attn: float32 [768], P('shard'), may hold values from -1.75 to 1.75
- w_qkv: float32 [768, 2304], P('shard'), may hold values from -0.3125 to 0.3125
- w_proj: float32 [768, 768], P('shard'), may hold values from -0.875 to 0.875
- gain_moe: float32 [768], P('shard'), may hold values from 0.5 to 1.5
- shift_moe: float32 [768], P('shard'), may hold values from -1.75 to 1.75
- w_router: float32 [768, 3], P('shard'), may hold values from -0.15625 to 0.15625
- w_in: float32 [768, 3, 3072], P('shard'), may hold values from -0.21875 to 0.21875
- w_out: float32 [3072, 3, 768], P('shard'), may hold values from -0.4375 to 0.4375
Outputs:
- output: bfloat16 [6304, 768], P(('shard', 'rep'))
- input_grad: bfloat16 [6304, 768], P(('shard', 'rep'))
- gain_attn_grad: float32 [768], P('shard')
- shift_attn_grad: float32 [768], P('shard')
- w_qkv_grad: float32 [768, 2304], P('shard')
- w_proj_grad: float32 [768, 768], P('shard')
- gain_moe_grad: float32 [768], P('shard')
- shift_moe_grad: float32 [768], P('shard')
- w_router_grad: float32 [768, 3], P('shard')
- w_in_grad: float32 [768, 3, 3072], P('shard')
- w_out_grad: float32 [3072, 3, 768], P('shard')
Inputs may be any that keep to these rules, and one draw needn't show every extreme that they name: `expert_index`: each row names two different experts. Where kept_mask is 1, slot_index counts the earlier assignments to the same expert among the rows of one device, all first choices of those rows counted before any second choice; where kept_mask is 0 it is 0. `kept_mask`: 1 exactly where that count is under 112; on every device some expert fills all 112 slots.
All inputs are finite; a program needn't handle non-finite values.
Results may differ from a plain program's by a relative error of at most 0.022.
Values may be sent and summed in bfloat16 or wider, within the bound.
A program may use at most 384 MiB of HBM per device.

v0:
```python
import jax
import jax.numpy as jnp
from jax import lax
from jax.sharding import PartitionSpec as P

HEADS = 12
HEAD_DIM = 64
SEQ = 197
CAP = 112


epsilon = 1e-06
score_scale = 0.125


def normalize(inputs):
    centred = inputs - jnp.mean(inputs, axis=-1, keepdims=True)
    inverse = lax.rsqrt(jnp.mean(centred * centred, axis=-1, keepdims=True) + epsilon)
    return (centred * inverse, inverse)


def norm_back(upstream, normed, inverse):
    return inverse * (
        upstream
        - jnp.mean(upstream, axis=-1, keepdims=True)
        - normed * jnp.mean(upstream * normed, axis=-1, keepdims=True)
    )


def to_heads(matrix, images):
    return matrix.reshape(images, -1, HEADS, HEAD_DIM)


def attn_weights_of(scores, log_total):
    return jnp.exp(scores - log_total)


def shards(
    tokens,
    cotangent,
    expert_index,
    slot_index,
    kept_mask,
    gain_attn,
    shift_attn,
    w_qkv,
    w_proj,
    gain_moe,
    shift_moe,
    w_router,
    w_in,
    w_out,
):
    model_width = tokens.shape[1]
    images = tokens.shape[0] // SEQ
    experts = w_in.shape[1]
    gain_first, shift_first, qkv_full, proj_full = (
        lax.all_gather(gain_attn.astype(jnp.bfloat16), "shard", axis=0, tiled=True),
        lax.all_gather(shift_attn.astype(jnp.bfloat16), "shard", axis=0, tiled=True),
        lax.all_gather(w_qkv.astype(jnp.bfloat16), "shard", axis=0, tiled=True),
        lax.all_gather(w_proj.astype(jnp.bfloat16), "shard", axis=0, tiled=True),
    )
    gain_second, shift_second, router_full, inner_full, outer_full = (
        lax.all_gather(gain_moe.astype(jnp.bfloat16), "shard", axis=0, tiled=True),
        lax.all_gather(shift_moe.astype(jnp.bfloat16), "shard", axis=0, tiled=True),
        lax.all_gather(w_router.astype(jnp.bfloat16), "shard", axis=0, tiled=True),
        lax.all_gather(w_in.astype(jnp.bfloat16), "shard", axis=0, tiled=True),
        lax.all_gather(w_out.astype(jnp.bfloat16), "shard", axis=0, tiled=True),
    )
    inputs = tokens.astype(jnp.float32)
    normed_one, inverse_one = normalize(inputs)
    ln_one = (normed_one * gain_first.astype(jnp.float32) + shift_first.astype(jnp.float32)).astype(
        jnp.bfloat16
    )
    triple = jnp.dot(ln_one, qkv_full, preferred_element_type=jnp.float32).astype(jnp.bfloat16)
    queries = to_heads(triple[:, :model_width], images)
    key_rows = to_heads(triple[:, model_width : 2 * model_width], images)
    value_rows = to_heads(triple[:, 2 * model_width :], images)
    scores = (
        jnp.einsum("ishd,ithd->ihst", queries, key_rows, preferred_element_type=jnp.float32)
        * score_scale
    )
    peak_score = jnp.max(scores, axis=-1, keepdims=True)
    log_total = peak_score + jnp.log(jnp.sum(jnp.exp(scores - peak_score), axis=-1, keepdims=True))
    attn_probs = attn_weights_of(scores, log_total)
    mixed_heads = (
        jnp.einsum(
            "ihst,ithd->ishd",
            attn_probs.astype(jnp.bfloat16),
            value_rows,
            preferred_element_type=jnp.float32,
        )
        .reshape(-1, model_width)
        .astype(jnp.bfloat16)
    )
    residual = inputs + jnp.dot(mixed_heads, proj_full, preferred_element_type=jnp.float32)
    normed_two, inverse_two = normalize(residual)
    ln_two = (
        normed_two * gain_second.astype(jnp.float32) + shift_second.astype(jnp.float32)
    ).astype(jnp.bfloat16)
    logits = jnp.dot(ln_two, router_full, preferred_element_type=jnp.float32)
    router_probs = jax.nn.softmax(logits, axis=-1)
    kept_float = kept_mask.astype(jnp.float32)
    choice_table = (
        expert_index[:, :, None] == jnp.arange(experts, dtype=jnp.int32)[None, None, :]
    ).astype(jnp.float32)
    gate_values = jnp.sum(choice_table * router_probs[:, None, :], axis=-1) * kept_float
    flat_slots = (expert_index * CAP + slot_index).reshape(-1)
    outgoing = (ln_two[:, None, :] * kept_mask[:, :, None].astype(jnp.bfloat16)).reshape(
        -1, model_width
    )
    dispatched = (
        jnp.zeros((experts * CAP, model_width), jnp.bfloat16)
        .at[flat_slots]
        .add(outgoing)
        .reshape(experts, CAP, model_width)
    )
    hidden_pre = jnp.einsum(
        "ecd,def->ecf", dispatched, inner_full, preferred_element_type=jnp.float32
    )
    active = jax.nn.gelu(hidden_pre).astype(jnp.bfloat16)
    expert_out = jnp.einsum(
        "ecf,fed->ecd", active, outer_full, preferred_element_type=jnp.float32
    ).reshape(-1, model_width)
    picked = expert_out[flat_slots].reshape(-1, 2, model_width)
    output = (residual + jnp.sum(gate_values[:, :, None] * picked, axis=1)).astype(jnp.bfloat16)
    gain_second, shift_second, router_full, inner_full, outer_full = (
        lax.all_gather(gain_moe.astype(jnp.bfloat16), "shard", axis=0, tiled=True),
        lax.all_gather(shift_moe.astype(jnp.bfloat16), "shard", axis=0, tiled=True),
        lax.all_gather(w_router.astype(jnp.bfloat16), "shard", axis=0, tiled=True),
        lax.all_gather(w_in.astype(jnp.bfloat16), "shard", axis=0, tiled=True),
        lax.all_gather(w_out.astype(jnp.bfloat16), "shard", axis=0, tiled=True),
    )
    upstream = cotangent.astype(jnp.float32)
    gate_grad = jnp.sum(upstream[:, None, :] * picked, axis=-1) * kept_float
    prob_grad = jnp.sum(choice_table * gate_grad[:, :, None], axis=1)
    logit_grad = (
        router_probs * (prob_grad - jnp.sum(router_probs * prob_grad, axis=-1, keepdims=True))
    ).astype(jnp.bfloat16)
    weighted = (gate_values[:, :, None] * upstream[:, None, :]).reshape(-1, model_width)
    outer_grad = (
        jnp.zeros((experts * CAP, model_width), jnp.float32)
        .at[flat_slots]
        .add(weighted)
        .astype(jnp.bfloat16)
        .reshape(experts, CAP, model_width)
    )
    outer_wgrad = jnp.einsum("ecf,ecd->fed", active, outer_grad, preferred_element_type=jnp.float32)
    active_grad = jnp.einsum(
        "ecd,fed->ecf", outer_grad, outer_full, preferred_element_type=jnp.float32
    )
    unused, gelu_pull = jax.vjp(jax.nn.gelu, hidden_pre)
    inner_grad = gelu_pull(active_grad)[0].astype(jnp.bfloat16)
    inner_wgrad = jnp.einsum(
        "ecd,ecf->def", dispatched, inner_grad, preferred_element_type=jnp.float32
    )
    slot_grad = jnp.einsum(
        "ecf,def->ecd", inner_grad, inner_full, preferred_element_type=jnp.float32
    ).reshape(-1, model_width)
    ln_two_grad = jnp.sum(
        slot_grad[flat_slots].reshape(-1, 2, model_width) * kept_float[:, :, None], axis=1
    )
    ln_two_grad = ln_two_grad + jnp.einsum(
        "te,de->td", logit_grad, router_full, preferred_element_type=jnp.float32
    )
    router_wgrad = jnp.einsum("td,te->de", ln_two, logit_grad, preferred_element_type=jnp.float32)
    gain_two_grad = jnp.sum(ln_two_grad * normed_two, axis=0)
    shift_two_grad = jnp.sum(ln_two_grad, axis=0)
    residual_grad = upstream + norm_back(
        ln_two_grad * gain_second.astype(jnp.float32), normed_two, inverse_two
    )
    owned_rows = w_in.shape[0]
    owned_hidden = w_out.shape[0]
    copies = lax.axis_size("rep")
    moe_shares = (
        lax.psum_scatter(
            gain_two_grad.astype(jnp.bfloat16), "shard", scatter_dimension=0, tiled=True
        ).astype(jnp.float32),
        lax.psum_scatter(
            shift_two_grad.astype(jnp.bfloat16), "shard", scatter_dimension=0, tiled=True
        ).astype(jnp.float32),
        lax.psum_scatter(
            router_wgrad.astype(jnp.bfloat16), "shard", scatter_dimension=0, tiled=True
        ).astype(jnp.float32),
        lax.psum_scatter(
            inner_wgrad.astype(jnp.bfloat16), "shard", scatter_dimension=0, tiled=True
        ).astype(jnp.float32),
        lax.psum_scatter(
            outer_wgrad.astype(jnp.bfloat16), "shard", scatter_dimension=0, tiled=True
        ).astype(jnp.float32),
    )
    small_shares = (moe_shares[0], moe_shares[1], moe_shares[2])
    rep_pair = (
        lax.psum_scatter(
            moe_shares[3].reshape(copies, -1).astype(jnp.bfloat16),
            "rep",
            scatter_dimension=0,
            tiled=True,
        ).astype(jnp.float32),
        lax.psum_scatter(
            moe_shares[4].reshape(copies, -1).astype(jnp.bfloat16),
            "rep",
            scatter_dimension=0,
            tiled=True,
        ).astype(jnp.float32),
    )
    rep_joined = (
        lax.all_gather(rep_pair[0].astype(jnp.bfloat16), "rep", axis=0, tiled=True).astype(
            jnp.float32
        ),
        lax.all_gather(rep_pair[1].astype(jnp.bfloat16), "rep", axis=0, tiled=True).astype(
            jnp.float32
        ),
    )
    inner_owned = rep_joined[0].reshape(owned_rows, experts, -1)
    outer_owned = rep_joined[1].reshape(owned_hidden, experts, -1)
    gain_first, shift_first, qkv_full, proj_full = (
        lax.all_gather(gain_attn.astype(jnp.bfloat16), "shard", axis=0, tiled=True),
        lax.all_gather(shift_attn.astype(jnp.bfloat16), "shard", axis=0, tiled=True),
        lax.all_gather(w_qkv.astype(jnp.bfloat16), "shard", axis=0, tiled=True),
        lax.all_gather(w_proj.astype(jnp.bfloat16), "shard", axis=0, tiled=True),
    )
    attn_grad = residual_grad.astype(jnp.bfloat16)
    proj_wgrad = jnp.einsum("tc,td->cd", mixed_heads, attn_grad, preferred_element_type=jnp.float32)
    mixed_grad = to_heads(
        jnp.einsum("td,cd->tc", attn_grad, proj_full, preferred_element_type=jnp.float32).astype(
            jnp.bfloat16
        ),
        images,
    )
    value_grad = jnp.einsum(
        "ihst,ishd->ithd",
        attn_probs.astype(jnp.bfloat16),
        mixed_grad,
        preferred_element_type=jnp.float32,
    )
    prob_attn_grad = jnp.einsum(
        "ishd,ithd->ihst", mixed_grad, value_rows, preferred_element_type=jnp.float32
    )
    score_grad = (
        attn_probs
        * (prob_attn_grad - jnp.sum(attn_probs * prob_attn_grad, axis=-1, keepdims=True))
        * score_scale
    ).astype(jnp.bfloat16)
    query_grad = jnp.einsum(
        "ihst,ithd->ishd", score_grad, key_rows, preferred_element_type=jnp.float32
    )
    key_grad = jnp.einsum(
        "ihst,ishd->ithd", score_grad, queries, preferred_element_type=jnp.float32
    )
    triple_grad = jnp.concatenate(
        [
            query_grad.reshape(-1, model_width),
            key_grad.reshape(-1, model_width),
            value_grad.reshape(-1, model_width),
        ],
        axis=1,
    ).astype(jnp.bfloat16)
    qkv_wgrad = jnp.einsum("tc,td->cd", ln_one, triple_grad, preferred_element_type=jnp.float32)
    ln_one_grad = jnp.einsum("td,cd->tc", triple_grad, qkv_full, preferred_element_type=jnp.float32)
    gain_one_grad = jnp.sum(ln_one_grad * normed_one, axis=0)
    shift_one_grad = jnp.sum(ln_one_grad, axis=0)
    input_grad = (
        residual_grad
        + norm_back(ln_one_grad * gain_first.astype(jnp.float32), normed_one, inverse_one)
    ).astype(jnp.bfloat16)
    attn_shares = (
        lax.psum_scatter(
            gain_one_grad.astype(jnp.bfloat16), "shard", scatter_dimension=0, tiled=True
        ).astype(jnp.float32),
        lax.psum_scatter(
            shift_one_grad.astype(jnp.bfloat16), "shard", scatter_dimension=0, tiled=True
        ).astype(jnp.float32),
        lax.psum_scatter(
            qkv_wgrad.astype(jnp.bfloat16), "shard", scatter_dimension=0, tiled=True
        ).astype(jnp.float32),
        lax.psum_scatter(
            proj_wgrad.astype(jnp.bfloat16), "shard", scatter_dimension=0, tiled=True
        ).astype(jnp.float32),
    )
    small_totals = (
        lax.psum(attn_shares[0].astype(jnp.bfloat16), "rep").astype(jnp.float32),
        lax.psum(attn_shares[1].astype(jnp.bfloat16), "rep").astype(jnp.float32),
        lax.psum(attn_shares[2].astype(jnp.bfloat16), "rep").astype(jnp.float32),
        lax.psum(attn_shares[3].astype(jnp.bfloat16), "rep").astype(jnp.float32),
        lax.psum(small_shares[0].astype(jnp.bfloat16), "rep").astype(jnp.float32),
        lax.psum(small_shares[1].astype(jnp.bfloat16), "rep").astype(jnp.float32),
        lax.psum(small_shares[2].astype(jnp.bfloat16), "rep").astype(jnp.float32),
    )
    return (
        output,
        input_grad,
        small_totals[0],
        small_totals[1],
        small_totals[2],
        small_totals[3],
        small_totals[4],
        small_totals[5],
        small_totals[6],
        inner_owned,
        outer_owned,
    )


def solution(mesh):
    return jax.shard_map(
        shards,
        mesh=mesh,
        in_specs=(
            P(("shard", "rep"), None),
            P(("shard", "rep"), None),
            P(("shard", "rep"), None),
            P(("shard", "rep"), None),
            P(("shard", "rep"), None),
            P("shard"),
            P("shard"),
            P("shard", None),
            P("shard", None),
            P("shard"),
            P("shard"),
            P("shard", None),
            P("shard", None, None),
            P("shard", None, None),
        ),
        out_specs=(
            P(("shard", "rep"), None),
            P(("shard", "rep"), None),
            P("shard"),
            P("shard"),
            P("shard", None),
            P("shard", None),
            P("shard"),
            P("shard"),
            P("shard", None),
            P("shard", None, None),
            P("shard", None, None),
        ),
        check_vma=False,
    )
```

profile of v0, /device:TPU:0, one launch (start us, length us, event | category | flops | bytes accessed | tf_op | source)
XLA Modules:
  0.0 967.8 jit_solution(10317299875728764457)
XLA Ops:
  19.7 15.6 %all-reduce.11 = (bf16[768]{0:T(1024)(128)(2,1)S(1)}, bf16[768]{0:T(1024)(128)(2,1)S(1)}, bf16[768]{0:T(1024)(128)(2,1)S(1)}, bf16[768]{0:T(1024)(128)(2,1)S(1)}) all-reduce(bf16[768]{0:T(1024)(128)(2,1)S(1)} %dynamic-update-slice.1, bf16[768]{0:T(1024)(128)(2,1)S(1)} %dynamic-update-slice, ...), channel_id=1, replica_groups=mesh['shard'=8,'rep'=4] {'shard'}, use_global_device_ids=true, to_apply=%add.1 | all-reduce | flops 3072 | bytes 12288
  40.1 7.9 all-gather
  58.8 15.1 %all-gather.12.cloned.1.call-done = bf16[768,768]{1,0:T(8,128)(2,1)} async-done(((bf16[96,768]{1,0:T(8,128)(2,1)}), bf16[768,768]{1,0:T(8,128)(2,1)}) %all-gather.12.cloned.1.call-update) | async-done | bytes 1179664 | tf_op jit(solution)/shard_map/all_gather | solution.py:61
  77.8 5.2 scatter_custom_fusion.1
  92.4 62.8 %all-gather.16.cloned.1.call-done = bf16[3072,3,768]{2,0,1:T(8,128)(2,1)} async-done(((bf16[384,3,768]{2,0,1:T(8,128)(2,1)}), bf16[3072,3,768]{2,0,1:T(8,128)(2,1)}) %all-gather.16.cloned.1.call-update) | async-done | bytes 14155792 | tf_op jit(solution)/shard_map/all_gather | solution.py:68
  155.2 11.5 %fusion.74 = f32[3,112,3072]{2,1,0:T(8,128)} fusion(bf16[3,112,768]{2,1,0:T(8,128)(2,1)S(1)} %bitcast.87, bf16[3072,3,768]{2,0,1:T(8,128)(2,1)} %all-gather.16.cloned.1.call-done), kind=kOutput, calls=%fused_computation.121 | convolution fusion | flops 1585446912 | bytes 18800640 | tf_op jit(solution)/shard_map/ecd,fed->ecf/dot_general | solution.py:149
  166.6 69.7 %all-gather.14.cloned.1.call-done = bf16[768,3,3072]{2,0,1:T(8,128)(2,1)} async-done(((bf16[96,3,3072]{2,0,1:T(8,128)(2,1)}), bf16[768,3,3072]{2,0,1:T(8,128)(2,1)}) %all-gather.14.cloned.1.call-update) | async-done | bytes 14155792 | tf_op jit(solution)/shard_map/all_gather | solution.py:67
  236.3 14.7 %fusion.7 = (bf16[3,112,3072]{2,1,0:T(8,128)(2,1)}, f32[3,112,3072]{2,1,0:T(8,128)}) fusion(f32[3,112,3072]{2,1,0:T(8,128)} %fusion.74, bf16[3,112,768]{2,1,0:T(8,128)(2,1)S(1)} %bitcast.95, bf16[768,3,3072]{2,0,1:T(8,128)(2,1)} %all-gather.14.cloned.1.call-done), kind=kOutput, calls=%fused_computation.16 | convolution fusion | flops 1606090752 | bytes 24993792 | tf_op jit(solution)/shard_map/ecd,def->ecf/dot_general | solution.py:118
  251.0 9.1 convolution_convert_fusion.1
  260.1 18.6 %copy.112 = bf16[768,9216]{1,0:T(8,128)(2,1)} copy(bf16[768,9216]{0,1:T(8,128)(2,1)} %bitcast.83) | data formatting | bytes 28311552
  278.8 11.0 %reduce-scatter.20.cloned.1.call-start = ((), (), s32[]{:S(2)}) async-start(), calls=%async_computation.15 | async-start | bytes 15925248
  289.8 11.6 %convolution_convert_fusion = bf16[3,768,3072]{2,1,0:T(8,128)(2,1)} fusion(bf16[3,112,768]{2,1,0:T(8,128)(2,1)S(1)} %bitcast.88, f32[3,112,3072]{2,1,0:T(8,128)} %get-tuple-element.87), kind=kOutput, calls=%fused_computation.5 | convolution fusion | flops 1601814528 | bytes 18800640 | tf_op jit(solution)/shard_map/ecf,ecd->fed/dot_general | solution.py:148
  301.3 18.2 %copy.114 = bf16[3072,2304]{1,0:T(8,128)(2,1)} copy(bf16[3072,2304]{0,1:T(8,128)(2,1)} %bitcast.84) | data formatting | bytes 28311552
  322.2 11.0 %fusion.75 = f32[3,112,768]{2,1,0:T(8,128)S(1)} fusion(bf16[3,112,3072]{2,1,0:T(8,128)(2,1)} %get-tuple-element.86, bf16[768,3,3072]{2,0,1:T(8,128)(2,1)} %all-gather.14.cloned.1.call-done), kind=kOutput, calls=%fused_computation.122 | convolution fusion | flops 1585446912 | bytes 17252352 | tf_op jit(solution)/shard_map/ecf,def->ecd/dot_general | solution.py:157
  338.5 9.0 fusion.68
  353.1 4.8 multiply_reduce_fusion.2
  391.1 5.7 convert_element_type.251
  396.8 87.1 %reduce-scatter.20.cloned.1.call-done = bf16[384,2304]{1,0:T(8,128)(2,1)} async-done(((bf16[3072,2304]{1,0:T(8,128)(2,1)}), bf16[384,2304]{1,0:T(8,128)(2,1)}) %reduce-scatter.20.cloned.1.call-update) | async-done | bytes 1769488
  494.5 29.4 %reduce-scatter.14.cloned.1.call-done = bf16[96,768]{1,0:T(8,128)(2,1)} async-done(((bf16[768,768]{1,0:T(8,128)(2,1)}), bf16[96,768]{1,0:T(8,128)(2,1)}) %reduce-scatter.14.cloned.1.call-update) | async-done | bytes 147472 | tf_op jit(solution)/shard_map/reduce_scatter | solution.py:277
  523.9 52.6 %reduce-scatter.12.cloned.1.call-done = bf16[96,2304]{1,0:T(8,128)(2,1)} async-done(((bf16[768,2304]{1,0:T(8,128)(2,1)}), bf16[96,2304]{1,0:T(8,128)(2,1)}) %reduce-scatter.12.cloned.1.call-update) | async-done | bytes 442384 | tf_op jit(solution)/shard_map/reduce_scatter | solution.py:274
  578.3 155.5 %all-reduce.16.cloned.1.call-done = (bf16[96,2304]{1,0:T(8,128)(2,1)}, bf16[96,768]{1,0:T(8,128)(2,1)}, bf16[4,221184]{1,0:T(4,128)(2,1)}, bf16[4,221184]{1,0:T(4,128)(2,1)}) async-done(((bf16[96,2304]{1,0:T(8,128)(2,1)}, bf16[96,768]{1,0:T(8,128)(2,1)}, bf16[4,221184]{1,0:T(4,128)(2,1)}, bf16[4,221184]{1,0:T(4,128)(2,1)}), (bf16[96,2304]{1,0:T(8,128)(2,1)}, bf16[96,768]{1,0:T(8,128)(2,1)}, ...) | async-done | bytes 4128784 | tf_op jit(solution)/shard_map/psum | solution.py:284
  744.5 14.0 %all-reduce.10 = (bf16[768]{0:T(1024)(128)(2,1)S(1)}, bf16[768]{0:T(1024)(128)(2,1)S(1)}, bf16[768]{0:T(1024)(128)(2,1)S(1)}, bf16[768]{0:T(1024)(128)(2,1)S(1)}) all-reduce(bf16[768]{0:T(1024)(128)(2,1)S(1)} %get-tuple-element.48, bf16[768]{0:T(1024)(128)(2,1)S(1)} %get-tuple-element.53, ...), channel_id=2, replica_groups=mesh['shard'=8,'rep'=4] {'shard'}, use_global_device_ids=true, to_apply=%region_22.0.clone | all-reduce | flops 3072 | bytes 12288
  759.8 9.9 %reduce-scatter.16.cloned.1.call-done = bf16[96,3]{1,0:T(8,128)(2,1)} async-done(((bf16[768,3]{1,0:T(8,128)(2,1)}), bf16[96,3]{1,0:T(8,128)(2,1)}) %reduce-scatter.16.cloned.1.call-update) | async-done | bytes 592
  770.6 11.9 %all-reduce.12 = (bf16[96]{0:T(256)(128)(2,1)S(1)}, bf16[96]{0:T(256)(128)(2,1)S(1)}, bf16[96]{0:T(256)(128)(2,1)S(1)}, bf16[96]{0:T(256)(128)(2,1)S(1)}, bf16[96,3]{0,1:T(4,128)(2,1)S(1)}) all-reduce(bf16[96]{0:T(256)(128)(2,1)S(1)} %dynamic-slice.5, bf16[96]{0:T(256)(128)(2,1)S(1)} %dynamic-slice.7, ...), channel_id=1, replica_groups=mesh['shard'=8,'rep'=4] {'rep'}, use_global_device_ids=true, to_apply=%region_23.0 | all-reduce | flops 672 | bytes 2688 | tf_op jit(solution)/shard_map/psum | solution.py:282
  786.8 55.3 %all-gather.18.cloned.1.call-done = bf16[4,1,221184]{2,1,0:T(2,128)(2,1)} async-done(((bf16[1,1,221184]{2,1,0:T(2,128)(2,1)}), bf16[4,1,221184]{2,1,0:T(2,128)(2,1)}) %all-gather.18.cloned.1.call-update) | async-done | bytes 1769488 | tf_op jit(solution)/shard_map/all_gather | solution.py:208
  842.0 38.2 %convert_reduce_fusion.1 = f32[4,221184]{1,0:T(4,128)S(1)} fusion(bf16[4,1,221184]{2,1,0:T(2,128)(2,1)} %all-gather.18.cloned.1.call-done), kind=kLoop, calls=%fused_computation.20 | loop fusion | flops 884736 | bytes 5308416 | tf_op jit(solution)/shard_map/reshape | solution.py:215
  880.3 5.4 reshape.275
  885.6 6.2 copy.100
  891.8 20.3 %all-gather.20.cloned.1.call-done = bf16[4,1,221184]{2,1,0:T(2,128)(2,1)} async-done(((bf16[1,1,221184]{2,1,0:T(2,128)(2,1)}), bf16[4,1,221184]{2,1,0:T(2,128)(2,1)}) %all-gather.20.cloned.1.call-update) | async-done | bytes 1769488 | tf_op jit(solution)/shard_map/all_gather | solution.py:211
  912.1 38.4 %convert_reduce_fusion = f32[4,221184]{1,0:T(4,128)S(1)} fusion(bf16[4,1,221184]{2,1,0:T(2,128)(2,1)} %all-gather.20.cloned.1.call-done), kind=kLoop, calls=%fused_computation.19 | loop fusion | flops 884736 | bytes 5308416 | tf_op jit(solution)/shard_map/reshape | solution.py:216
  950.6 5.3 reshape.277
  955.9 4.8 copy.101
  (280 shorter events, 115.3 us)
Async XLA Ops:
  7.2 43.9 %all-gather.10.cloned.1.call-start = ((), (), s32[]{:S(2)}) async-start(), calls=%async_computation.5 | async-start | bytes 3981312 | tf_op jit(solution)/shard_map/all_gather | solution.py:60
  9.2 64.6 %all-gather.12.cloned.1.call-start = ((), (), s32[]{:S(2)}) async-start(), calls=%async_computation.6 | async-start | bytes 1327104 | tf_op jit(solution)/shard_map/all_gather | solution.py:61
  11.0 144.2 %all-gather.16.cloned.1.call-start = ((), (), s32[]{:S(2)}) async-start(), calls=%async_computation.8 | async-start | bytes 15925248 | tf_op jit(solution)/shard_map/all_gather | solution.py:68
  14.6 20.8 %copy-start.43 = (s32[197,2]{0,1:T(2,128)S(1)}, s32[197,2]{0,1:T(2,128)}, u32[]{:S(2)}) copy-start(s32[197,2]{0,1:T(2,128)} %param.16) | copy-start | bytes 4732
  14.6 221.7 %all-gather.14.cloned.1.call-start = ((), (), s32[]{:S(2)}) async-start(), calls=%async_computation.7 | async-start | bytes 15925248 | tf_op jit(solution)/shard_map/all_gather | solution.py:67
  16.1 24.0 %copy-start.65 = (f32[96,3]{0,1:T(4,128)S(1)}, f32[96,3]{0,1:T(4,128)}, u32[]{:S(2)}) copy-start(f32[96,3]{0,1:T(4,128)} %param.25) | copy-start | bytes 3460
  16.2 32.6 %copy-start.40 = (s32[197,2]{0,1:T(2,128)S(1)}, s32[197,2]{0,1:T(2,128)}, u32[]{:S(2)}) copy-start(s32[197,2]{0,1:T(2,128)} %param.18) | copy-start | bytes 4732
  16.2 34.0 %copy-start.4 = (bf16[197,768]{1,0:T(8,128)(2,1)S(1)}, bf16[197,768]{1,0:T(8,128)(2,1)}, u32[]{:S(2)}) copy-start(bf16[197,768]{1,0:T(8,128)(2,1)} %param.14) | copy-start | bytes 907780
  16.2 368.3 %reduce-scatter.18.cloned.1.call-start = ((), (), s32[]{:S(2)}) async-start(), calls=%async_computation.14 | async-start | bytes 15925248
  35.4 40.6 %copy-start.28 = (f32[768]{0:T(1024)}, f32[768]{0:T(1024)S(1)}, u32[]{:S(2)}) copy-start(f32[768]{0:T(1024)S(1)} %convert_element_type.216) | copy-start | bytes 9220
  58.8 17.7 %copy-start.50 = (f32[768]{0:T(1024)S(1)}, f32[768]{0:T(1024)}, u32[]{:S(2)}) copy-start(f32[768]{0:T(1024)} %convert_element_type.218) | copy-start | bytes 9220
  58.8 17.9 %copy-start.32 = (bf16[768,3]{0,1:T(4,128)(2,1)S(1)}, bf16[768,3]{0,1:T(4,128)(2,1)}, u32[]{:S(2)}) copy-start(bf16[768,3]{0,1:T(4,128)(2,1)} %reshape.323) | copy-start | bytes 13828
  58.8 18.2 %copy-start.44 = (s32[197,2]{0,1:T(2,128)S(1)}, s32[197,2]{0,1:T(2,128)}, u32[]{:S(2)}) copy-start(s32[197,2]{0,1:T(2,128)} %param.16) | copy-start | bytes 4732
  58.8 18.2 %copy-start.41 = (s32[197,2]{0,1:T(2,128)S(1)}, s32[197,2]{0,1:T(2,128)}, u32[]{:S(2)}) copy-start(s32[197,2]{0,1:T(2,128)} %param.18) | copy-start | bytes 4732
  76.9 285.0 %copy-start.34 = (f32[197]{0:T(256)}, f32[197]{0:T(256)S(1)}, u32[]{:S(2)}) copy-start(f32[197]{0:T(256)S(1)} %get-tuple-element.84) | copy-start | bytes 2368
  77.0 284.9 %copy-start.38 = (f32[197]{0:T(256)}, f32[197]{0:T(256)S(1)}, u32[]{:S(2)}) copy-start(f32[197]{0:T(256)S(1)} %fusion.55) | copy-start | bytes 2368
  278.8 205.1 %reduce-scatter.20.cloned.1.call-start = ((), (), s32[]{:S(2)}) async-start(), calls=%async_computation.15 | async-start | bytes 15925248
  319.6 204.4 %reduce-scatter.14.cloned.1.call-start = ((), (), s32[]{:S(2)}) async-start(), calls=%async_computation.10 | async-start | bytes 1327104 | tf_op jit(solution)/shard_map/reduce_scatter | solution.py:277
  366.3 210.2 %reduce-scatter.12.cloned.1.call-start = ((), (), s32[]{:S(2)}) async-start(), calls=%async_computation.9 | async-start | bytes 3981312 | tf_op jit(solution)/shard_map/reduce_scatter | solution.py:274
  384.5 349.3 %all-reduce.16.cloned.1.call-start = ((), (), s32[]{:S(2)}) async-start(), calls=%async_computation.16 | async-start | bytes 8257536 | tf_op jit(solution)/shard_map/psum | solution.py:284
  494.5 82.1 %copy-start.71 = (u32[32]{0:T(128)S(1)}, u32[32]{0:T(128)}, u32[]{:S(2)}) copy-start(u32[32]{0:T(128)} %constant.89) | copy-start | bytes 388
  494.5 82.7 %copy-start.7 = (bf16[197,768]{1,0:T(8,128)(2,1)S(1)}, bf16[197,768]{1,0:T(8,128)(2,1)}, u32[]{:S(2)}) copy-start(bf16[197,768]{1,0:T(8,128)(2,1)} %copy-done.6) | copy-start | bytes 907780
  494.5 82.7 %copy-start.31 = (f32[197,3]{0,1:T(4,128)S(1)}, f32[197,3]{0,1:T(4,128)}, u32[]{:S(2)}) copy-start(f32[197,3]{0,1:T(4,128)} %copy-done.30) | copy-start | bytes 7096
  494.5 82.7 %copy-start.35 = (f32[197]{0:T(256)S(1)}, f32[197]{0:T(256)}, u32[]{:S(2)}) copy-start(f32[197]{0:T(256)} %copy-done.34) | copy-start | bytes 2368
  494.5 82.7 %copy-start.39 = (f32[197]{0:T(256)S(1)}, f32[197]{0:T(256)}, u32[]{:S(2)}) copy-start(f32[197]{0:T(256)} %copy-done.38) | copy-start | bytes 2368
  494.5 82.7 %copy-start.54 = (f32[197]{0:T(256)S(1)}, f32[197]{0:T(256)}, u32[]{:S(2)}) copy-start(f32[197]{0:T(256)} %copy-done.53) | copy-start | bytes 2368
  576.5 193.2 %reduce-scatter.16.cloned.1.call-start = ((), (), s32[]{:S(2)}) async-start(), calls=%async_computation.13 | async-start | bytes 221184
  578.2 263.8 %all-gather.18.cloned.1.call-start = ((), (), s32[]{:S(2)}) async-start(), calls=%async_computation.11 | async-start | bytes 4423680 | tf_op jit(solution)/shard_map/all_gather | solution.py:208
  737.5 174.6 %all-gather.20.cloned.1.call-start = ((), (), s32[]{:S(2)}) async-start(), calls=%async_computation.12 | async-start | bytes 4423680 | tf_op jit(solution)/shard_map/all_gather | solution.py:211
  740.7 18.2 %copy-start.3 = (f32[197,768]{1,0:T(8,128)S(1)}, f32[197,768]{1,0:T(8,128)}, u32[]{:S(2)}) copy-start(f32[197,768]{1,0:T(8,128)} %copy-done.2) | copy-start | bytes 1815556
  740.7 44.4 %copy-start.21 = (bf16[96,2304]{1,0:T(8,128)(2,1)S(1)}, bf16[96,2304]{1,0:T(8,128)(2,1)}, u32[]{:S(2)}) copy-start(bf16[96,2304]{1,0:T(8,128)(2,1)} %get-tuple-element.67) | copy-start | bytes 1327108
  744.5 41.5 %copy-start.27 = (bf16[96,768]{1,0:T(8,128)(2,1)S(1)}, bf16[96,768]{1,0:T(8,128)(2,1)}, u32[]{:S(2)}) copy-start(bf16[96,768]{1,0:T(8,128)(2,1)} %get-tuple-element.68) | copy-start | bytes 442372
  (52 other events, 251.3 us)
Sparse Core Ops, SparseCore 0:
  10.5 36.8 all-gather.9
  49.8 24.0 all-gather.11
  76.4 78.7 all-gather.15
  157.5 78.7 all-gather.13
  278.9 100.7 reduce-scatter.17
  383.1 100.7 reduce-scatter.19
  487.1 36.7 reduce-scatter.13
  528.4 48.0 reduce-scatter.11
  579.9 153.8 all-reduce.15
  737.2 32.4 reduce-scatter.15
  772.0 69.9 all-gather.17
  843.5 68.5 all-gather.19
where the time goes:
time: 978 us; the launch traced here: 968 us
  waiting for transfers between devices  558 us (57%)
  local copies, waits for them, and re-layouts  119 us (12%)
  other arithmetic  116 us (12%)
  matrix products  97 us (10%)
  blocking collectives  49.4 us (5%)
  between operations  16.8 us (2%)
  starting transfers between devices  11.8 us (1%)
    psum x1, waiting for transfers between devices, shards(): lax.psum(attn_shares[2].astype(jnp.bfloat16), 'rep').astype(jnp.float32)  156 us
    unnamed x15, waiting for transfers between devices  97.2 us
    unnamed x169, local copies, waits for them, and re-layouts  69.8 us
    all_gather x1, waiting for transfers between devices, shards(): lax.all_gather(w_in.astype(jnp.bfloat16), 'shard', axis=0, tiled=True)  69.7 us
    all_gather x1, waiting for transfers between devices, shards(): lax.all_gather(w_out.astype(jnp.bfloat16), 'shard', axis=0, tiled=True)  62.8 us
    all_gather x1, waiting for transfers between devices, shards(): lax.all_gather(rep_pair[0].astype(jnp.bfloat16), 'rep', axis=0, tiled=True)  55.3 us
    reduce_scatter x1, waiting for transfers between devices, shards(): lax.psum_scatter(qkv_wgrad.astype(jnp.bfloat16), 'shard', scatter_dimensi...  52.6 us
    reshape x1, other arithmetic, shards(): outer_owned = rep_joined[1].reshape(owned_hidden, experts, -1)  38.4 us
  transfers between devices with their start and end apart: 12, of which 10 were waited for; matrix products, arithmetic and copies ran while one was open for 24% of the time, Pallas kernels for 0%

commit v1 on v0

v1 whole, which is shorter than its diff:
```python
import jax
import jax.numpy as jnp
from jax import lax
from jax.sharding import PartitionSpec as P

HEADS = 12
HEAD_DIM = 64
SEQ = 197
CAP = 112


epsilon = 1e-06
score_scale = 0.125


def normalize(inputs):
    centred = inputs - jnp.mean(inputs, axis=-1, keepdims=True)
    inverse = lax.rsqrt(jnp.mean(centred * centred, axis=-1, keepdims=True) + epsilon)
    return (centred * inverse, inverse)


def norm_back(upstream, normed, inverse):
    return inverse * (
        upstream
        - jnp.mean(upstream, axis=-1, keepdims=True)
        - normed * jnp.mean(upstream * normed, axis=-1, keepdims=True)
    )


def to_heads(matrix, images):
    return matrix.reshape(images, -1, HEADS, HEAD_DIM)


def shards(
    tokens,
    cotangent,
    expert_index,
    slot_index,
    kept_mask,
    gain_attn,
    shift_attn,
    w_qkv,
    w_proj,
    gain_moe,
    shift_moe,
    w_router,
    w_in,
    w_out,
):
    model_width = tokens.shape[1]
    images = tokens.shape[0] // SEQ
    rows = tokens.shape[0]
    experts = w_in.shape[1]
    group = lax.axis_size("shard")
    low = jnp.bfloat16
    wide = jnp.float32

    def gathered(value):
        return lax.all_gather(value, "shard", axis=0, tiled=True)

    qkv_full = gathered(w_qkv.astype(low))
    proj_full = gathered(w_proj.astype(low))
    smalls = gathered(
        jnp.concatenate(
            [
                jnp.stack([gain_attn, shift_attn, gain_moe, shift_moe], axis=1),
                w_router,
            ],
            axis=1,
        ).astype(low)
    )
    gain_first, shift_first, gain_second, shift_second = (
        smalls[:, index].astype(wide) for index in range(4)
    )
    router_full = smalls[:, 4:]
    inner_part = lax.all_to_all(w_in.astype(low), "shard", split_axis=2, concat_axis=0, tiled=True)
    outer_part = w_out.astype(low)
    upstream_all = gathered(cotangent).reshape(group, rows, model_width)
    flat_slots = jnp.where(kept_mask == 1, expert_index * CAP + slot_index, -1)
    slots_all = gathered(flat_slots).reshape(group, rows, 2)
    slot_numbers = jnp.arange(experts * CAP, dtype=jnp.int32)
    picks = slots_all[:, None, :, :] == slot_numbers[None, :, None, None]
    placed = jnp.any(picks, axis=-1)
    placed_low = placed.astype(low)

    inputs = tokens.astype(wide)
    normed_one, inverse_one = normalize(inputs)
    ln_one = (normed_one * gain_first + shift_first).astype(low)
    triple = jnp.dot(ln_one, qkv_full, preferred_element_type=wide).astype(low)
    queries = to_heads(triple[:, :model_width], images)
    key_rows = to_heads(triple[:, model_width : 2 * model_width], images)
    value_rows = to_heads(triple[:, 2 * model_width :], images)
    scores = (
        jnp.einsum("ishd,ithd->ihst", queries, key_rows, preferred_element_type=wide) * score_scale
    )
    attn_probs = jax.nn.softmax(scores, axis=-1)
    mixed_heads = (
        jnp.einsum(
            "ihst,ithd->ishd", attn_probs.astype(low), value_rows, preferred_element_type=wide
        )
        .reshape(-1, model_width)
        .astype(low)
    )
    residual = inputs + jnp.dot(mixed_heads, proj_full, preferred_element_type=wide)
    normed_two, inverse_two = normalize(residual)
    ln_two = (normed_two * gain_second + shift_second).astype(low)
    ln_two_all = gathered(ln_two).reshape(group, rows, model_width)
    logits = jnp.einsum("btd,de->bte", ln_two_all, router_full, preferred_element_type=wide)
    probs_all = jax.nn.softmax(logits, axis=-1)
    me = lax.axis_index("shard")
    router_probs = lax.dynamic_index_in_dim(probs_all, me, 0, keepdims=False)
    placed_own = lax.dynamic_index_in_dim(placed, me, 0, keepdims=False).astype(wide)
    probs_slots = jnp.repeat(jnp.transpose(probs_all, (0, 2, 1)), CAP, axis=1)
    gate_slots = jnp.sum(placed.astype(wide) * probs_slots, axis=-1)

    def to_slots(values):
        return jnp.einsum("bst,btd->bsd", placed_low, values, preferred_element_type=wide)

    def to_experts(values):
        width = values.shape[-1]
        return jnp.transpose(values.reshape(group, experts, CAP, width), (1, 0, 2, 3)).reshape(
            experts, group * CAP, width
        )

    def from_experts(values):
        width = values.shape[-1]
        return jnp.transpose(values.reshape(experts, group, CAP, width), (1, 0, 2, 3)).reshape(
            group, experts * CAP, width
        )

    def to_tokens(values):
        return jnp.einsum("bst,bsd->btd", placed_low, values, preferred_element_type=wide)

    dispatched = to_experts(to_slots(ln_two_all).astype(low))
    upstream_slots = to_slots(upstream_all)
    outer_grad = to_experts((upstream_slots * gate_slots[:, :, None]).astype(low))
    hidden_pre = jnp.einsum("ecd,def->ecf", dispatched, inner_part, preferred_element_type=wide)
    hidden_act, gelu_pull = jax.vjp(jax.nn.gelu, hidden_pre)
    active = hidden_act.astype(low)
    outer_wgrad = jnp.einsum("ecf,ecd->fed", active, outer_grad, preferred_element_type=wide)
    outer_owned = lax.psum(outer_wgrad.astype(low), "rep").astype(wide)
    active_grad = jnp.einsum("ecd,fed->ecf", outer_grad, outer_part, preferred_element_type=wide)
    inner_grad = gelu_pull(active_grad)[0].astype(low)
    inner_wgrad = jnp.einsum("ecd,ecf->def", dispatched, inner_grad, preferred_element_type=wide)
    inner_rows = lax.all_to_all(
        inner_wgrad.astype(low).reshape(group, -1, experts, inner_part.shape[2]),
        "shard",
        split_axis=0,
        concat_axis=0,
        tiled=True,
    )
    slot_grad = from_experts(
        jnp.einsum("ecf,def->ecd", inner_grad, inner_part, preferred_element_type=wide).astype(low)
    )

    def scattered(values):
        return lax.psum_scatter(values, "shard", scatter_dimension=0, tiled=True)

    raise_grad = scattered(to_tokens(slot_grad).astype(low).reshape(-1, model_width)).astype(wide)
    expert_out = from_experts(
        jnp.einsum("ecf,fed->ecd", active, outer_part, preferred_element_type=wide)
    )
    mixture = scattered(
        to_tokens((expert_out * gate_slots[:, :, None]).astype(low))
        .astype(low)
        .reshape(-1, model_width)
    )
    output = (residual + mixture.astype(wide)).astype(low)
    gate_part = scattered(jnp.sum(expert_out * upstream_slots, axis=-1)).reshape(experts * CAP)
    prob_grad = jnp.transpose(
        jnp.sum((placed_own * gate_part[:, None]).reshape(experts, CAP, rows), axis=1)
    )
    upstream = cotangent.astype(wide)
    logit_grad = (
        router_probs * (prob_grad - jnp.sum(router_probs * prob_grad, axis=-1, keepdims=True))
    ).astype(low)
    ln_two_grad = raise_grad + jnp.einsum(
        "te,de->td", logit_grad, router_full, preferred_element_type=wide
    )
    router_wgrad = jnp.einsum("td,te->de", ln_two, logit_grad, preferred_element_type=wide)
    gain_two_grad = jnp.sum(ln_two_grad * normed_two, axis=0)
    shift_two_grad = jnp.sum(ln_two_grad, axis=0)
    residual_grad = upstream + norm_back(ln_two_grad * gain_second, normed_two, inverse_two)
    attn_grad = residual_grad.astype(low)
    proj_wgrad = jnp.einsum("tc,td->cd", mixed_heads, attn_grad, preferred_element_type=wide)
    mixed_grad = to_heads(
        jnp.einsum("td,cd->tc", attn_grad, proj_full, preferred_element_type=wide).astype(low),
        images,
    )
    value_grad = jnp.einsum(
        "ihst,ishd->ithd", attn_probs.astype(low), mixed_grad, preferred_element_type=wide
    )
    prob_attn_grad = jnp.einsum(
        "ishd,ithd->ihst", mixed_grad, value_rows, preferred_element_type=wide
    )
    score_grad = (
        attn_probs
        * (prob_attn_grad - jnp.sum(attn_probs * prob_attn_grad, axis=-1, keepdims=True))
        * score_scale
    ).astype(low)
    query_grad = jnp.einsum("ihst,ithd->ishd", score_grad, key_rows, preferred_element_type=wide)
    key_grad = jnp.einsum("ihst,ishd->ithd", score_grad, queries, preferred_element_type=wide)
    triple_grad = jnp.concatenate(
        [
            query_grad.reshape(-1, model_width),
            key_grad.reshape(-1, model_width),
            value_grad.reshape(-1, model_width),
        ],
        axis=1,
    ).astype(low)
    qkv_wgrad = jnp.einsum("tc,td->cd", ln_one, triple_grad, preferred_element_type=wide)
    ln_one_grad = jnp.einsum("td,cd->tc", triple_grad, qkv_full, preferred_element_type=wide)
    gain_one_grad = jnp.sum(ln_one_grad * normed_one, axis=0)
    shift_one_grad = jnp.sum(ln_one_grad, axis=0)
    input_grad = (
        residual_grad + norm_back(ln_one_grad * gain_first, normed_one, inverse_one)
    ).astype(low)
    small_grads = jnp.concatenate(
        [
            jnp.stack([gain_one_grad, shift_one_grad, gain_two_grad, shift_two_grad], axis=1),
            router_wgrad,
        ],
        axis=1,
    )
    attn_shares = scattered(jnp.concatenate([qkv_wgrad, proj_wgrad, small_grads], axis=1).astype(low))
    inner_flat, attn_total = lax.psum((inner_rows, attn_shares), "rep")
    inner_owned = jnp.transpose(inner_flat.astype(wide), (1, 2, 0, 3)).reshape(w_in.shape)
    attn_total = attn_total.astype(wide)
    wide_end = w_qkv.shape[1]
    small_end = wide_end + model_width
    return (
        output,
        input_grad,
        attn_total[:, small_end],
        attn_total[:, small_end + 1],
        attn_total[:, :wide_end],
        attn_total[:, wide_end:small_end],
        attn_total[:, small_end + 2],
        attn_total[:, small_end + 3],
        attn_total[:, small_end + 4 :],
        inner_owned,
        outer_owned,
    )


def solution(mesh):
    return jax.shard_map(
        shards,
        mesh=mesh,
        in_specs=(
            P(("shard", "rep"), None),
            P(("shard", "rep"), None),
            P(("shard", "rep"), None),
            P(("shard", "rep"), None),
            P(("shard", "rep"), None),
            P("shard"),
            P("shard"),
            P("shard", None),
            P("shard", None),
            P("shard"),
            P("shard"),
            P("shard", None),
            P("shard", None, None),
            P("shard", None, None),
        ),
        out_specs=(
            P(("shard", "rep"), None),
            P(("shard", "rep"), None),
            P("shard"),
            P("shard"),
            P("shard", None),
            P("shard", None),
            P("shard"),
            P("shard"),
            P("shard", None),
            P("shard", None, None),
            P("shard", None, None),
        ),
        check_vma=False,
    )
```

time: 978 us -> 568 us (0.58)
  waiting for transfers between devices: 558 us -> 242 us
  other arithmetic: 116 us -> 19.4 us
  blocking collectives: 49.4 us -> 133 us
  local copies, waits for them, and re-layouts: 119 us -> 59.6 us
  matrix products: 97 us -> 78.5 us
    all_gather x6 -> x4, waiting for transfers between devices: 223 us -> 41.5 us  [gathered(): return lax.all_gather(value, 'shard', axis=0, tiled=True)]
    unnamed x15 -> x8, waiting for transfers between devices: 97.2 us -> 0.61 us
    reshape x2 -> x1, other arithmetic: 76.7 us -> 2.21 us  [shards(): jnp.transpose(inner_flat.astype(wide), (1, 2, 0, 3)).reshape(w_in.shape)]
    reduce_scatter x2 -> x1, waiting for transfers between devices: 82 us -> 15.8 us  [scattered(): return lax.psum_scatter(values, 'shard', scatter_dimension=0, tiled=True)]
    unnamed x169 -> x107, local copies, waits for them, and re-layouts: 69.8 us -> 15 us
    all_gather x1 -> x2, blocking collectives: 7.88 us -> 57.2 us  [gathered(): return lax.all_gather(value, 'shard', axis=0, tiled=True)]
    unnamed x2, blocking collectives: 29.6 us -> 75.8 us
    all_to_all x0 -> x2, waiting for transfers between devices: none -> 27.2 us  [the longest x1 27.2 us: shards(): lax.all_to_all(inner_wgrad.astype(low).reshape(group, -1, experts, inner_...]
  transfers between devices with their start and end apart: 12 -> 10, of which waited for: 10 -> 5; matrix products, arithmetic and copies ran while one was open for 24% -> 14% of each run, Pallas kernels for 0% -> 0%
where the time goes in v1:
time: 568 us; the launch traced here: 563 us
  waiting for transfers between devices  242 us (43%)
  blocking collectives  133 us (23%)
  matrix products  78.5 us (14%)
  local copies, waits for them, and re-layouts  59.6 us (10%)
  other arithmetic  19.4 us (3%)
  between operations  15.9 us (3%)
  starting transfers between devices  14.4 us (3%)
    psum x1, waiting for transfers between devices, shards(): outer_owned = lax.psum(outer_wgrad.astype(low), 'rep').astype(wide)  157 us
    unnamed x2, blocking collectives  75.8 us
    all_gather x2, blocking collectives, gathered(): return lax.all_gather(value, 'shard', axis=0, tiled=True)  57.2 us
    all_gather x4, waiting for transfers between devices, gathered(): return lax.all_gather(value, 'shard', axis=0, tiled=True)  41.5 us
    all_to_all x1, waiting for transfers between devices, shards(): lax.all_to_all(inner_wgrad.astype(low).reshape(group, -1, experts, inner_...  27.2 us
    reduce_scatter x1, waiting for transfers between devices, scattered(): return lax.psum_scatter(values, 'shard', scatter_dimension=0, tiled=True)  15.8 us
    unnamed x107, local copies, waits for them, and re-layouts  15 us
  transfers between devices with their start and end apart: 10, of which 5 were waited for; matrix products, arithmetic and copies ran while one was open for 14% of the time, Pallas kernels for 0%

profile of v1, /device:TPU:0, one launch (start us, length us, event | category | flops | bytes accessed | tf_op | source)
XLA Modules:
  0.0 562.7 jit_solution(11165241325182985829)
XLA Ops:
  13.1 10.3 %all-gather = bf16[8,96,7]{1,2,0:T(8,128)(2,1)S(1)} all-gather(bf16[1,96,7]{1,2,0:T(8,128)(2,1)S(1)} %bitcast.157), channel_id=1, replica_groups=mesh['shard'=8,'rep'=4] {'shard'}, dimensions={0}, use_global_device_ids=true | all-gather | bytes 12096 | tf_op jit(solution)/shard_map/all_gather | solution.py:59
  24.0 23.1 %all-gather.9.cloned.1.call-done = bf16[768,2304]{1,0:T(8,128)(2,1)} async-done(((bf16[96,2304]{1,0:T(8,128)(2,1)}), bf16[768,2304]{1,0:T(8,128)(2,1)}) %all-gather.9.cloned.1.call-update) | async-done | bytes 3538960 | tf_op jit(solution)/shard_map/all_gather | solution.py:59
  47.2 3.0 convolution_convert_fusion.1
  55.4 18.3 %all-gather.11.cloned.1.call-done = bf16[768,768]{1,0:T(8,128)(2,1)} async-done(((bf16[96,768]{1,0:T(8,128)(2,1)}), bf16[768,768]{1,0:T(8,128)(2,1)}) %all-gather.11.cloned.1.call-update) | async-done | bytes 1179664 | tf_op jit(solution)/shard_map/all_gather | solution.py:59
  79.6 3.6 copy.189
  83.1 4.6 all-to-all-start
  88.4 46.9 %all-gather.1 = s32[8,197,2]{1,2,0:T(2,128)S(1)} all-gather(s32[1,197,2]{1,2,0:T(2,128)S(1)} %fusion.86), channel_id=1, replica_groups=mesh['shard'=8,'rep'=4] {'shard'}, dimensions={0}, use_global_device_ids=true | all-gather | bytes 14184 | tf_op jit(solution)/shard_map/all_gather | solution.py:59
  138.5 4.4 copy.190
  142.9 3.1 convolution_convert_fusion.3
  150.6 2.6 fusion.41
  153.2 3.7 copy.191
  156.9 2.5 fusion.101
  161.2 3.5 copy.192
  166.8 6.3 %fusion.21 = bf16[8,197,768]{2,1,0:T(8,128)(2,1)} fusion(f32[8,336,768]{2,1,0:T(8,128)} %bitcast.128, f32[8,336]{1,0:T(8,128)S(1)} %select_reduce_fusion, pred[8,336,197]{1,0,2:T(8,128)(4,1)S(1)} %fusion.5), kind=kOutput, calls=%fused_computation.31 | convolution fusion | flops 818706432 | bytes 11218560 | tf_op jit(solution)/shard_map/bst,bsd->btd/dot_general | solution.py:132
  173.1 3.9 reshape.258
  177.1 6.3 %multiply_reduce_fusion = (f32[8,336]{1,0:T(8,128)S(1)}, bf16[8,336,768]{2,1,0:T(8,128)(2,1)S(1)}) fusion(f32[8,336,768]{2,1,0:T(8,128)} %bitcast.129, f32[8,336]{1,0:T(8,128)S(1)} %select_reduce_fusion, bf16[8,197,768]{2,1,0:T(8,128)(2,1)} %all-gather.15.cloned.1.call-done, pred[8,336,197]{1,0,2:T(8,128)(4,1)S(1)} %fusion.5), kind=kOutput, calls=%fused_computation.3 | convolution fusion | flops 821622144 | bytes 15358080 | tf_op jit(solution)/shard_map/bst,btd->bsd/dot_general | solution.py:117
  183.8 3.3 copy-done.1
  188.1 4.2 fusion.12
  198.6 52.4 %fusion.96 = (bf16[200,768]{1,0:T(8,128)(2,1)S(1)}, bf16[200,768]{1,0:T(8,128)(2,1)S(1)}) fusion(bf16[1576,768]{1,0:T(8,128)(2,1)} %reshape.258, bf16[1576,768]{1,0:T(8,128)(2,1)} %reshape.264), kind=kCustom, calls=%all-reduce-scatter.2 | all-reduce-scatter fusion | flops 2457601 | bytes 5456384
  252.4 23.5 %all-reduce.2 = f32[8,336]{1,0:T(8,128)S(1)} all-reduce(f32[8,336]{1,0:T(8,128)S(1)} %get-tuple-element.100), channel_id=4, replica_groups=mesh['shard'=8,'rep'=4] {'shard'}, use_global_device_ids=true, to_apply=%region_13.14.clone | all-reduce | flops 2688 | bytes 21504
  290.9 5.5 fusion.31
  296.5 5.6 fusion.28
  302.6 4.4 convolution_convert_fusion
  309.9 8.2 %concatenate.14 = bf16[768,3079]{1,0:T(8,128)(2,1)} concatenate(bf16[768,2304]{1,0:T(8,128)(2,1)} %convolution_convert_fusion, bf16[768,768]{1,0:T(8,128)(2,1)S(1)} %convolution_convert_fusion.5, bf16[768,1]{1,0:T(8,128)(2,1)S(1)} %stack.40, bf16[768,1]{1,0:T(8,128)(2,1)S(1)} %stack.41, bf16[768,1]{1,0:T(8,128)(2,1)S(1)} %stack.42, bf16[768,1]{1,0:T(8,128)(2,1)S(1)} %stack.43, ...), dimensions={1} | concatenate | bytes 9458688 | tf_op jit(solution)/shard_map/concatenate | solution.py:225
  319.6 5.5 convert_bitcast_fusion.1
  325.1 2.8 copy.210
  329.3 6.1 %all-to-all-start.1 = ((bf16[8,96,3,384]{3,1,2,0:T(8,128)(2,1)}), bf16[8,96,3,384]{3,1,2,0:T(8,128)(2,1)S(1)}, u32[]{:S(2)}, u32[]{:S(2)}) async-start(bf16[8,96,3,384]{3,1,2,0:T(8,128)(2,1)} %copy.211), calls=%async_computation.2 | async-start | bytes 3538944 | tf_op jit(solution)/shard_map/all_to_all | solution.py:145
  335.6 7.4 %convert_bitcast_fusion = bf16[384,3,768]{0,2,1:T(8,128)(2,1)} fusion(bf16[3,896,768]{2,1,0:T(8,128)(2,1)} %bitcast.144, f32[3,896,384]{2,1,0:T(8,128)} %copy-done), kind=kOutput, calls=%fused_computation.35 | convolution fusion | flops 1595621376 | bytes 10027008 | tf_op jit(solution)/shard_map/ecf,ecd->fed/dot_general | solution.py:140
  343.0 27.2 %all-to-all-done.1 = bf16[8,96,3,384]{3,1,2,0:T(8,128)(2,1)S(1)} async-done(((bf16[8,96,3,384]{3,1,2,0:T(8,128)(2,1)}), bf16[8,96,3,384]{3,1,2,0:T(8,128)(2,1)S(1)}, u32[]{:S(2)}, u32[]{:S(2)}) %all-to-all-start.1) | async-done | bytes 1769504 | tf_op jit(solution)/shard_map/all_to_all | solution.py:145
  371.8 15.8 %reduce-scatter.6.cloned.1.call-done = bf16[96,3079]{1,0:T(8,128)(2,1)} async-done(((bf16[768,3079]{1,0:T(8,128)(2,1)}), bf16[96,3079]{1,0:T(8,128)(2,1)}) %reduce-scatter.6.cloned.1.call-update) | async-done | bytes 591184 | tf_op jit(solution)/shard_map/reduce_scatter | solution.py:157
  388.6 156.6 %all-reduce.9.cloned.1.call-done = (bf16[384,3,768]{0,2,1:T(8,128)(2,1)}, bf16[96,3079]{1,0:T(8,128)(2,1)}, bf16[96,3,3072]{2,0,1:T(8,128)(2,1)}) async-done(((bf16[384,3,768]{0,2,1:T(8,128)(2,1)}, bf16[96,3079]{1,0:T(8,128)(2,1)}, bf16[96,3,3072]{2,0,1:T(8,128)(2,1)}), (bf16[384,3,768]{0,2,1:T(8,128)(2,1)}, bf16[96,3079]{1,0:T(8,128)(2,1)}, bf16[96,3,3072]{2,0,1:T(8,128)(2,1)})) %all-reduce.9.cloned.1.call-update) | async-done | bytes 4130128 | tf_op jit(solution)/shard_map/psum | solution.py:141
  553.0 2.6 copy.215
  (194 shorter events, 69.6 us)
Async XLA Ops:
  7.2 16.4 %copy-start.6 = (bf16[197,768]{1,0:T(8,128)(2,1)S(1)}, bf16[197,768]{1,0:T(8,128)(2,1)}, u32[]{:S(2)}) copy-start(bf16[197,768]{1,0:T(8,128)(2,1)} %param.14) | copy-start | bytes 907780
  7.2 40.0 %all-gather.9.cloned.1.call-start = ((), (), s32[]{:S(2)}) async-start(), calls=%async_computation.3 | async-start | bytes 3981312 | tf_op jit(solution)/shard_map/all_gather | solution.py:59
  9.3 64.5 %all-gather.11.cloned.1.call-start = ((), (), s32[]{:S(2)}) async-start(), calls=%async_computation.4 | async-start | bytes 1327104 | tf_op jit(solution)/shard_map/all_gather | solution.py:59
  11.0 131.9 %all-gather.13.cloned.1.call-start = ((), (), s32[]{:S(2)}) async-start(), calls=%async_computation.6 | async-start | bytes 2764800 | tf_op jit(solution)/shard_map/all_gather | solution.py:59
  23.6 26.6 %copy-start.28 = (f32[768]{0:T(1024)}, f32[768]{0:T(1024)S(1)}, u32[]{:S(2)}) copy-start(f32[768]{0:T(1024)S(1)} %get-tuple-element.92) | copy-start | bytes 9220
  23.6 26.6 %copy-start.38 = (f32[768]{0:T(1024)}, f32[768]{0:T(1024)S(1)}, u32[]{:S(2)}) copy-start(f32[768]{0:T(1024)S(1)} %get-tuple-element.91) | copy-start | bytes 9220
  23.6 52.2 %copy-start.30 = (f32[768]{0:T(1024)}, f32[768]{0:T(1024)S(1)}, u32[]{:S(2)}) copy-start(f32[768]{0:T(1024)S(1)} %get-tuple-element.90) | copy-start | bytes 9220
  23.8 26.4 %copy-start.32 = (f32[197]{0:T(256)}, f32[197]{0:T(256)S(1)}, u32[]{:S(2)}) copy-start(f32[197]{0:T(256)S(1)} %broadcast_multiply_fusion.5) | copy-start | bytes 2368
  24.0 26.2 %copy-start.36 = (f32[197]{0:T(256)}, f32[197]{0:T(256)S(1)}, u32[]{:S(2)}) copy-start(f32[197]{0:T(256)S(1)} %add_rsqrt_fusion.1) | copy-start | bytes 2368
  55.4 21.9 %copy-start.17 = (bf16[12,64,197]{2,1,0:T(8,128)(2,1)}, bf16[12,64,197]{2,1,0:T(8,128)(2,1)S(1)}, u32[]{:S(2)}) copy-start(bf16[12,64,197]{2,1,0:T(8,128)(2,1)S(1)} %convolution_convert_fusion.7) | copy-start | bytes 907780
  83.1 54.1 %copy-start.43 = (u32[32]{0:T(128)S(1)}, u32[32]{0:T(128)}, u32[]{:S(2)}) copy-start(u32[32]{0:T(128)} %constant.65) | copy-start | bytes 388
  83.1 55.3 %all-to-all-start = ((bf16[96,3,3072]{0,1,2:T(4,128)(2,1)}), bf16[96,3,3072]{0,1,2:T(4,128)(2,1)}, u32[]{:S(2)}, u32[]{:S(2)}) async-start(bf16[96,3,3072]{0,1,2:T(4,128)(2,1)} %copy.189), calls=%async_computation | async-start | bytes 6291456 | tf_op jit(solution)/shard_map/all_to_all | solution.py:76
  87.8 89.3 %all-gather.15.cloned.1.call-start = ((), (), s32[]{:S(2)}) async-start(), calls=%async_computation.7 | async-start | bytes 2764800 | tf_op jit(solution)/shard_map/all_gather | solution.py:59
  88.3 299.2 %reduce-scatter.6.cloned.1.call-start = ((), (), s32[]{:S(2)}) async-start(), calls=%async_computation.5 | async-start | bytes 5529600 | tf_op jit(solution)/shard_map/reduce_scatter | solution.py:157
  183.7 8.6 %copy-start.8 = (bf16[8,3,112,768]{3,2,0,1:T(8,128)(2,1)}, bf16[8,3,112,768]{3,2,0,1:T(8,128)(2,1)S(1)}, u32[]{:S(2)}) copy-start(bf16[8,3,112,768]{3,2,0,1:T(8,128)(2,1)S(1)} %copy.195) | copy-start | bytes 12386308
  198.6 80.2 %copy-start.4 = (f32[197,768]{1,0:T(8,128)S(1)}, f32[197,768]{1,0:T(8,128)}, u32[]{:S(2)}) copy-start(f32[197,768]{1,0:T(8,128)} %copy-done.3) | copy-start | bytes 1815556
  198.6 80.2 %copy-start.27 = (f32[197]{0:T(256)S(1)}, f32[197]{0:T(256)}, u32[]{:S(2)}) copy-start(f32[197]{0:T(256)} %copy-done.26) | copy-start | bytes 2368
  198.6 80.2 %copy-start.31 = (f32[768]{0:T(1024)S(1)}, f32[768]{0:T(1024)}, u32[]{:S(2)}) copy-start(f32[768]{0:T(1024)} %copy-done.30) | copy-start | bytes 9220
  198.6 80.2 %copy-start.35 = (f32[197]{0:T(256)S(1)}, f32[197]{0:T(256)}, u32[]{:S(2)}) copy-start(f32[197]{0:T(256)} %copy-done.34) | copy-start | bytes 2368
  251.0 32.8 %copy-start.19 = (bf16[197,768]{1,0:T(8,128)(2,1)S(1)}, bf16[197,768]{1,0:T(8,128)(2,1)}, u32[]{:S(2)}) copy-start(bf16[197,768]{1,0:T(8,128)(2,1)} %param.15) | copy-start | bytes 907780
  251.0 28.9 %collective-permute-start.1 = (bf16[21,768]{1,0:T(8,128)(2,1)S(1)}, bf16[21,768]{1,0:T(8,128)(2,1)S(1)}, u32[]{:S(2)}, u32[]{:S(2)}) collective-permute-start(bf16[21,768]{1,0:T(8,128)(2,1)S(1)} %slice.76), channel_id=1, source_target_pairs={{0,4},{4,8},{8,12},{12,16},{16,20},{20,24},{24,28},{1,5},{5,9},{9,... | collective-permute-start | bytes 96776
  276.7 5.8 %collective-permute-start = (bf16[21,768]{1,0:T(8,128)(2,1)S(1)}, bf16[21,768]{1,0:T(8,128)(2,1)}, u32[]{:S(2)}, u32[]{:S(2)}) collective-permute-start(bf16[21,768]{1,0:T(8,128)(2,1)S(1)} %slice.75), channel_id=1, source_target_pairs={{0,4},{4,8},{8,12},{12,16},{16,20},{20,24},{24,28},{1,5},{5,9},{9,... | collective-permute-start | bytes 96776
  290.9 5.5 copy-start.25
  296.4 5.6 copy-start.18
  296.4 6.1 %copy-start.29 = (f32[768]{0:T(1024)S(1)}, f32[768]{0:T(1024)}, u32[]{:S(2)}) copy-start(f32[768]{0:T(1024)} %copy-done.28) | copy-start | bytes 9220
  296.4 6.1 %copy-start.33 = (f32[197]{0:T(256)S(1)}, f32[197]{0:T(256)}, u32[]{:S(2)}) copy-start(f32[197]{0:T(256)} %copy-done.32) | copy-start | bytes 2368
  296.4 6.1 %copy-start.37 = (f32[197]{0:T(256)S(1)}, f32[197]{0:T(256)}, u32[]{:S(2)}) copy-start(f32[197]{0:T(256)} %copy-done.36) | copy-start | bytes 2368
  296.5 6.1 %copy-start.39 = (f32[768]{0:T(1024)S(1)}, f32[768]{0:T(1024)}, u32[]{:S(2)}) copy-start(f32[768]{0:T(1024)} %copy-done.38) | copy-start | bytes 9220
  329.3 40.9 %all-to-all-start.1 = ((bf16[8,96,3,384]{3,1,2,0:T(8,128)(2,1)}), bf16[8,96,3,384]{3,1,2,0:T(8,128)(2,1)S(1)}, u32[]{:S(2)}, u32[]{:S(2)}) async-start(bf16[8,96,3,384]{3,1,2,0:T(8,128)(2,1)} %copy.211), calls=%async_computation.2 | async-start | bytes 3538944 | tf_op jit(solution)/shard_map/all_to_all | solution.py:145
  335.4 209.9 %all-reduce.9.cloned.1.call-start = ((), (), s32[]{:S(2)}) async-start(), calls=%async_computation.8 | async-start | bytes 8306688 | tf_op jit(solution)/shard_map/psum | solution.py:141
  371.8 15.9 %copy-start.21 = (f32[197,768]{1,0:T(8,128)S(1)}, f32[197,768]{1,0:T(8,128)}, u32[]{:S(2)}) copy-start(f32[197,768]{1,0:T(8,128)} %get-tuple-element.116) | copy-start | bytes 1815556
  545.3 5.5 copy-start.14
  (27 other events, 91.9 us)
Sparse Core Ops, SparseCore 0:
  10.5 36.6 all-gather.8
  49.6 24.0 all-gather.10
  77.4 46.2 all-gather.12
  125.4 36.6 all-gather.14
  318.2 69.3 reduce-scatter.5
  390.8 154.4 all-reduce.8

commit v2 on v1

--- a/solution.py
+++ b/solution.py
@@ -1,7 +1,12 @@
 import jax
 import jax.numpy as jnp
 from jax import lax
+from jax.experimental import pallas as pl
+from jax.experimental.pallas import tpu as pltpu
 from jax.sharding import PartitionSpec as P
+
+MESH = pl.DeviceIdType.MESH
+VMEM_BYTES = 64 * 1024 * 1024 - 256 * 1024
 
 HEADS = 12
 HEAD_DIM = 64
@@ -243,9 +248,816 @@
     )
 
 
+TILE_ROWS = 256
+SENT_ROWS = 208
+TABLE_ROW = 200
+PIECE = 96
+NEGATIVE = -1e30
+
+
+def mega(
+    tok_ref,
+    ups_ref,
+    small_ref,
+    qkv_ref,
+    proj_ref,
+    inner_hbm,
+    outer_ref,
+    out_ref,
+    igrad_ref,
+    go_hbm,
+    gi_hbm,
+    ga_hbm,
+    smalls,
+    small_sum,
+    wq,
+    wp,
+    win,
+    normed_a,
+    inv_a,
+    ln_a,
+    tri,
+    probs,
+    heads,
+    resid,
+    mean_m,
+    inv_m,
+    rows_buf,
+    onehot,
+    work,
+    og,
+    route,
+    act,
+    slope,
+    route_grad,
+    st_back,
+    sr_back,
+    rr_back,
+    sr_out,
+    rr_out,
+    grad_in,
+    grad_in_own,
+    grad_out,
+    grad_attn,
+    mid_in,
+    mid_out,
+    mid_attn,
+    end_in,
+    end_out,
+    end_attn,
+    res_grad,
+    agrad,
+    mgrad,
+    small_grad,
+    small_swap,
+    send_sems,
+    recv_sems,
+    local_sems,
+):
+    low = jnp.bfloat16
+    wide = jnp.float32
+    width = tok_ref.shape[1]
+    shard = lax.axis_index("shard")
+    rep = lax.axis_index("rep")
+
+    def flip(j):
+        out = shard
+        for bit in range(3):
+            if (j >> bit) & 1:
+                out = out + (1 - 2 * ((shard // (1 << bit)) % 2)) * (1 << bit)
+        return out
+
+    peers = [flip(j) for j in range(8)]
+    pair = rep + 1 - 2 * (rep % 2)
+    across = 3 - rep
+    is_mid = jnp.logical_and(rep >= 1, rep <= 2)
+    is_end = jnp.logical_not(is_mid)
+
+    ups_base = 8 * TILE_ROWS
+    for position in range(16):
+        rows_buf[pl.ds(position * TILE_ROWS + SENT_ROWS, TILE_ROWS - SENT_ROWS), :] = jnp.zeros(
+            (TILE_ROWS - SENT_ROWS, width), low
+        )
+    barrier = pltpu.get_barrier_semaphore()
+    for j in range(1, 8):
+        pl.semaphore_signal(barrier, inc=1, device_id=(peers[j], rep), device_id_type=MESH)
+    pl.semaphore_signal(barrier, inc=1, device_id=(shard, pair), device_id_type=MESH)
+
+    @pl.when(is_mid)
+    def _():
+        pl.semaphore_signal(barrier, inc=1, device_id=(shard, across), device_id_type=MESH)
+        pl.semaphore_wait(barrier, 9)
+
+    @pl.when(is_end)
+    def _():
+        pl.semaphore_wait(barrier, 8)
+
+    count = [0]
+    unsent = []
+    settled = []
+
+    def describe(src, dst, device):
+        index = count[0]
+        count[0] += 1
+        return pltpu.make_async_remote_copy(
+            src_ref=src,
+            dst_ref=dst,
+            send_sem=send_sems.at[index],
+            recv_sem=recv_sems.at[index],
+            device_id=device,
+            device_id_type=MESH,
+        )
+
+    def send(src, dst, j):
+        copy = describe(src, dst, (peers[j], rep))
+        copy.start()
+        unsent.append(copy)
+        return copy
+
+    def settle(copies):
+        for copy in copies:
+            copy.wait_send()
+            settled.append(id(copy))
+
+    local_count = [0]
+
+    def local(src, dst):
+        copy = pltpu.make_async_copy(src, dst, local_sems.at[local_count[0]])
+        local_count[0] += 1
+        copy.start()
+        return copy
+
+    def off(value, unit):
+        return pl.multiple_of(value * unit, unit)
+
+    class Gather:
+        def __init__(self, view, first, second):
+            self.view, self.first, self.second = view, first, second
+            self.all = []
+
+        def put(self, at, to, j, half=None):
+            copy = send(self.view(at, at, half), self.view(at, to, half), j)
+            self.all.append(copy)
+            return copy
+
+        def begin(self):
+            self.from_x = self.put(0, 2, 2)
+            self.from_y = self.put(0, 4, 4)
+            self.from_s = [self.put(0, 1, 1)]
+
+        def pass_on(self):
+            self.from_x.wait_recv()
+            self.far = [self.put(2, 6, 4, self.first)]
+            self.from_s.append(self.put(2, 3, 1))
+            self.from_y.wait_recv()
+            self.far.append(self.put(4, 6, 2, self.second))
+            self.from_s.append(self.put(4, 5, 1))
+
+        def last(self):
+            for copy in self.far:
+                copy.wait_recv()
+            self.from_s.append(self.put(6, 7, 1))
+
+    def weight_view(ref):
+        def view(at, to, half):
+            start = off(peers[at], PIECE)
+            if half is None:
+                return ref.at[pl.ds(start, PIECE)]
+            return ref.at[pl.ds(start + half[0], half[1])]
+
+        return view
+
+    def row_view(base):
+        def view(at, to, half):
+            first, size = half if half is not None else (0, SENT_ROWS)
+            return rows_buf.at[pl.ds(base + to * TILE_ROWS + first, size)]
+
+        return view
+
+    own_rows = pl.ds(off(shard, PIECE), PIECE)
+    small_copies = []
+    smalls[0] = small_ref[...]
+    for j in range(1, 8):
+        small_copies.append(send(smalls.at[0], smalls.at[j], j))
+    wq[own_rows, :] = qkv_ref[...].astype(low)
+    gather_q = Gather(weight_view(wq), (0, 48), (48, 48))
+    gather_q.begin()
+    wp[own_rows, :] = proj_ref[...].astype(low)
+    rows_buf[ups_base : ups_base + SENT_ROWS, :] = ups_ref[...]
+    inputs = tok_ref[...].astype(wide)
+    normed, inverse = normalize(inputs)
+    normed_a[...] = normed
+    inv_a[...] = inverse
+    gather_q.pass_on()
+    gather_p = Gather(weight_view(wp), (0, 48), (48, 48))
+    gather_p.begin()
+    part = win.shape[2]
+    inner_copies = [
+        send(
+            inner_hbm.at[:, :, pl.ds(off(peers[j], part), part)],
+            win.at[:, own_rows, :],
+            j,
+        )
+        for j in range(1, 8)
+    ]
+    inner_own = local(inner_hbm.at[:, :, pl.ds(off(shard, part), part)], win.at[:, own_rows, :])
+    gather_u = Gather(row_view(ups_base), (0, 112), (112, 96))
+    gather_u.begin()
+    for copy in small_copies:
+        copy.wait_recv()
+    total = smalls[0].astype(wide)
+    for j in range(1, 8):
+        total = total + smalls[j].astype(wide)
+    small_sum[...] = total
+    gain_first, shift_first = small_sum[3:4, :], small_sum[4:5, :]
+    gain_second, shift_second = small_sum[5:6, :], small_sum[6:7, :]
+    ln_a[...] = (normed_a[...] * gain_first + shift_first).astype(low)
+    gather_q.last()
+    for copy in gather_q.from_s:
+        copy.wait_recv()
+
+    def triple_step(i, carry):
+        columns = pl.ds(off(i, 384), 384)
+        tri[:, columns] = jnp.dot(
+            ln_a[...], wq[:, columns], preferred_element_type=wide
+        ).astype(low)
+        return carry
+
+    lax.fori_loop(0, 6, triple_step, 0)
+
+    lane = lax.broadcasted_iota(jnp.int32, (TILE_ROWS, 128), 1)
+    key_at = lax.broadcasted_iota(jnp.int32, (TILE_ROWS, TILE_ROWS), 1)
+
+    def head_columns(p, third):
+        return pl.ds(pl.multiple_of(third * width + p * 128, 128), 128)
+
+    def contract(a, b, da, db):
+        return lax.dot_general(a, b, (((da,), (db,)), ((), ())), preferred_element_type=wide)
+
+    def one_head(values, side):
+        return jnp.where((lane < 64) == (side == 0), values, jnp.zeros_like(values))
+
+    def attend(p, carry):
+        queries = tri[:, head_columns(p, 0)]
+        key_rows = tri[:, head_columns(p, 1)]
+        value_rows = tri[:, head_columns(p, 2)]
+        mixed = []
+        for side in range(2):
+            scores = contract(one_head(queries, side), key_rows, 1, 1) * score_scale
+            scores = jnp.where(key_at < SEQ, scores, NEGATIVE)
+            powers = jnp.exp(scores - jnp.max(scores, axis=-1, keepdims=True))
+            weights = powers / jnp.sum(powers, axis=-1, keepdims=True)
+            probs[2 * p + side] = weights
+            mixed.append(jnp.dot(weights.astype(low), value_rows, preferred_element_type=wide))
+        heads[:, head_columns(p, 0)] = jnp.where(lane < 64, mixed[0], mixed[1]).astype(low)
+        return carry
+
+    lax.fori_loop(0, 3, attend, 0)
+    gather_p.pass_on()
+    lax.fori_loop(3, 6, attend, 0)
+    gather_u.pass_on()
+    gather_p.last()
+    for copy in gather_p.from_s:
+        copy.wait_recv()
+    residual = tok_ref[...].astype(wide) + jnp.dot(
+        heads[...], wp[...], preferred_element_type=wide
+    )
+    resid[...] = residual
+    normed, inverse = normalize(residual)
+    mean_m[...] = jnp.mean(residual, axis=-1, keepdims=True)
+    inv_m[...] = inverse
+    ln_two = (normed * gain_second + shift_second).astype(low)
+    rows_buf[0:SENT_ROWS, :] = ln_two[0:SENT_ROWS, :]
+    gather_l = Gather(row_view(0), (0, 112), (112, 96))
+    gather_l.begin()
+    gather_u.last()
+    for copy in gather_u.from_s:
+        copy.wait_recv()
+
+    slots = onehot.shape[1]
+    slot_at = lax.broadcasted_iota(jnp.int32, (slots, TILE_ROWS), 0).astype(wide)
+
+    def route_step(j, carry):
+        start = pl.multiple_of(ups_base + j * TILE_ROWS + 192, 16)
+        table = rows_buf[pl.ds(start, 16), :].astype(wide)
+        first = table[8:9, 0:256] * CAP + table[8:9, 256:512]
+        second = table[9:10, 0:256] * CAP + table[9:10, 256:512]
+        hit = jnp.logical_or(slot_at == first, slot_at == second)
+        onehot[j] = jnp.where(hit, 1.0, 0.0).astype(low)
+        return carry
+
+    lax.fori_loop(0, 8, route_step, 0)
+    router = small_sum[...].astype(low)
+    lane16 = lax.broadcasted_iota(jnp.int32, (slots, 16), 1)
+    expert_of = lax.broadcasted_iota(jnp.int32, (slots, 16), 0)
+    own_lane = jnp.logical_and(expert_of >= lane16 * CAP, expert_of < lane16 * CAP + CAP)
+    experts = win.shape[0]
+
+    def expert_rows(e, j, blocks=1):
+        return pl.ds(pl.multiple_of((e * 8 + j) * CAP, 16), blocks * CAP)
+
+    def dispatch_step(j, carry):
+        picks = onehot[j]
+        ln_rows = rows_buf[pl.ds(off(j, TILE_ROWS), TILE_ROWS), :]
+        up_rows = rows_buf[pl.ds(pl.multiple_of(ups_base + j * TILE_ROWS, 16), TILE_ROWS), :]
+        sent = jnp.dot(picks, ln_rows, preferred_element_type=wide).astype(low)
+        logits = jnp.where(lane16 < experts, contract(sent, router, 1, 1), NEGATIVE)
+        powers = jnp.exp(logits - jnp.max(logits, axis=-1, keepdims=True))
+        chances = powers / jnp.sum(powers, axis=-1, keepdims=True)
+        gate = jnp.sum(jnp.where(own_lane, chances, 0.0), axis=-1, keepdims=True)
+        ups = jnp.dot(picks, up_rows, preferred_element_type=wide)
+        upward = (ups * gate).astype(low)
+        for e in range(experts):
+            rows = expert_rows(e, j)
+            work[rows, :] = sent[e * CAP : (e + 1) * CAP]
+            og[rows, :] = upward[e * CAP : (e + 1) * CAP]
+            route[rows, :] = chances[e * CAP : (e + 1) * CAP]
+        return carry
+
+    def hidden_step(g):
+        def step(e, carry):
+            rows = pl.ds(g * 2 * CAP, 2 * CAP)
+            sent = work[expert_rows(e, 2 * g, 2), :]
+            value = jnp.dot(sent, win[e], preferred_element_type=wide)
+            square = value * value
+            bend = jnp.tanh(0.7978845608028654 * value * (1.0 + 0.044715 * square))
+            act[e, rows, :] = (0.5 * value * (1.0 + bend)).astype(low)
+            slope[e, rows, :] = (
+                0.5 * (1.0 + bend)
+                + 0.5
+                * value
+                * (1.0 - bend * bend)
+                * (0.7978845608028654 * (1.0 + 0.134145 * square))
+            ).astype(low)
+            return carry
+
+        lax.fori_loop(0, experts, step, 0)
+
+    inner_own.wait()
+    for copy in inner_copies:
+        copy.wait_recv()
+    gather_l.pass_on()
+    gather_l.from_s[0].wait_recv()
+    lax.fori_loop(0, 2, dispatch_step, 0)
+    hidden_step(0)
+    gather_l.last()
+    for g in range(1, 4):
+        gather_l.from_s[g].wait_recv()
+        lax.fori_loop(2 * g, 2 * g + 2, dispatch_step, 0)
+        hidden_step(g)
+
+    class Copies:
+        def __init__(self, own, mid, end, out, rows):
+            self.own, self.mid, self.end, self.out, self.rows = own, mid, end, out, rows
+            self.up = describe(own, end, (shard, pair))
+            self.over = describe(own, mid, (shard, across))
+            self.down = describe(end, end, (shard, pair))
+
+        def add(self, target, other):
+            size = self.rows
+
+            def step(i, carry):
+                at = pl.ds(pl.multiple_of(i * size, 16), size)
+                target[at, :] = (
+                    self.own[at, :].astype(wide) + other[at, :].astype(wide)
+                ).astype(low)
+                return carry
+
+            lax.fori_loop(0, target.shape[0] // size, step, 0)
+
+        def rise(self):
+            @pl.when(is_end)
+            def _():
+                self.up.start()
+
+        def cross(self):
+            @pl.when(is_mid)
+            def _():
+                self.up.wait_recv()
+                self.add(self.own, self.end)
+                self.over.start()
+
+        def fall(self):
+            @pl.when(is_mid)
+            def _():
+                self.over.wait_recv()
+                self.add(self.end, self.mid)
+                self.down.start()
+
+        def finish(self):
+            @pl.when(is_end)
+            def _():
+                self.up.wait_send()
+                self.down.wait_recv()
+
+            write = local(self.end, self.out)
+
+            @pl.when(is_mid)
+            def _():
+                self.over.wait_send()
+                self.down.wait_send()
+
+            write.wait()
+
+    out_copies = [
+        Copies(grad_out.at[e], mid_out.at[e], end_out.at[e], go_hbm.at[e], 64) for e in range(experts)
+    ]
+    in_copies = [
+        Copies(grad_in_own.at[e], mid_in.at[e], end_in.at[e], gi_hbm.at[e], 16)
+        for e in range(experts)
+    ]
+    attn_copies = Copies(grad_attn, mid_attn, end_attn, ga_hbm, 80)
+
+    for e in range(experts):
+        grad_out[e] = contract(act[e], og[expert_rows(e, 0, 8), :], 0, 0).astype(low)
+        out_copies[e].rise()
+
+    settle(gather_l.all)
+    settle(gather_u.all)
+    route_grad[...] = jnp.zeros(route_grad.shape, wide)
+    half = act.shape[1] // 2
+    lane_h = lax.broadcasted_iota(jnp.int32, (half, 16), 1)
+
+    def back_step(i, carry):
+        e = i // 2
+        rows = pl.ds(off(i % 2, half), half)
+        flat = pl.ds(pl.multiple_of(i * half, 16), half)
+        upward = og[flat, :]
+        gone = jnp.dot(act[e, rows, :], outer_ref[e], preferred_element_type=wide)
+        chances = route[flat, :]
+        gate = jnp.sum(jnp.where(lane_h == e, chances, 0.0), axis=-1, keepdims=True)
+        pull = jnp.sum(upward.astype(wide) * gone, axis=-1, keepdims=True)
+        logit = (pull * (jnp.where(lane_h == e, 1.0, 0.0) - chances)).astype(low)
+        logit = jnp.where(lane_h < experts, logit, jnp.zeros_like(logit))
+        rows_buf[flat, :] = (gone * gate).astype(low)
+        inner = contract(upward, outer_ref[e], 1, 1) * slope[e, rows, :].astype(wide)
+        inner = inner.astype(low)
+        slope[e, rows, :] = inner
+        og[flat, :] = (
+            contract(inner, win[e], 1, 1) + jnp.dot(logit, router, preferred_element_type=wide)
+        ).astype(low)
+        route_grad[...] += contract(logit, work[flat, :], 0, 0)
+        return carry
+
+    lax.fori_loop(0, 2 * experts, back_step, 0)
+
+    def combine_back(j):
+        joined = jnp.concatenate([og[expert_rows(e, j), :] for e in range(experts)], axis=0)
+        return contract(onehot[j], joined, 0, 0)[0:SENT_ROWS]
+
+    def combine_out(j):
+        joined = jnp.concatenate(
+            [rows_buf[expert_rows(e, j), :] for e in range(experts)], axis=0
+        )
+        return contract(onehot[j], joined, 0, 0)[0:SENT_ROWS]
+
+    stage_out = experts * 8 * CAP
+
+    def odd_back(i, carry):
+        st_back[i] = combine_back(2 * i + 1).astype(low)
+        return carry
+
+    lax.fori_loop(0, 4, odd_back, 0)
+    swap_back = send(st_back, sr_back, 1)
+
+    def inner_grad_step(e, carry):
+        grad_in[e] = contract(work[expert_rows(e, 0, 8), :], slope[e], 0, 0).astype(low)
+        return carry
+
+    lax.fori_loop(0, experts, inner_grad_step, 0)
+    swap_back.wait_recv()
+
+    def even_back(i, carry):
+        sr_back[i] = (combine_back(2 * i) + sr_back[i].astype(wide)).astype(low)
+        return carry
+
+    lax.fori_loop(0, 4, even_back, 0)
+    back_copies = [send(sr_back.at[i], rr_back.at[i - 1], 2 * i) for i in range(1, 4)]
+    grad_in_copies = [
+        send(
+            grad_in.at[:, pl.ds(off(peers[j], PIECE), PIECE), :],
+            grad_in_own.at[:, :, pl.ds(off(shard, part), part)],
+            j,
+        )
+        for j in range(1, 8)
+    ]
+    grad_in_local = local(
+        grad_in.at[:, own_rows, :], grad_in_own.at[:, :, pl.ds(off(shard, part), part)]
+    )
+
+    def odd_out(i, carry):
+        rows = pl.ds(pl.multiple_of(stage_out + i * SENT_ROWS, 16), SENT_ROWS)
+        rows_buf[rows, :] = combine_out(2 * i + 1).astype(low)
+        return carry
+
+    lax.fori_loop(0, 4, odd_out, 0)
+    swap_out = send(rows_buf.at[pl.ds(stage_out, 4 * SENT_ROWS)], sr_out, 1)
+    out_copies[0].cross()
+    swap_out.wait_recv()
+
+    def even_out(i, carry):
+        rows = pl.ds(off(i, SENT_ROWS), SENT_ROWS)
+        sr_out[rows, :] = (combine_out(2 * i) + sr_out[rows, :].astype(wide)).astype(low)
+        return carry
+
+    lax.fori_loop(0, 4, even_out, 0)
+
+    for copy in back_copies:
+        copy.wait_recv()
+    out_sends = [
+        send(sr_out.at[pl.ds(i * SENT_ROWS, SENT_ROWS)], rr_out.at[i - 1], 2 * i)
+        for i in range(1, 4)
+    ]
+    ln_grad = sr_back[0].astype(wide)
+    for i in range(3):
+        ln_grad = ln_grad + rr_back[i].astype(wide)
+    normed = (resid[0:SENT_ROWS, :] - mean_m[0:SENT_ROWS, :]) * inv_m[0:SENT_ROWS, :]
+    gain_m_grad = jnp.sum(ln_grad * normed, axis=0, keepdims=True)
+    shift_m_grad = jnp.sum(ln_grad, axis=0, keepdims=True)
+    upstream = jnp.where(
+        lax.broadcasted_iota(jnp.int32, (SENT_ROWS, width), 0) < SEQ,
+        ups_ref[...].astype(wide),
+        0.0,
+    )
+    residual_grad = upstream + norm_back(
+        ln_grad * gain_second, normed, inv_m[0:SENT_ROWS, :]
+    )
+    res_grad[...] = residual_grad
+    agrad[...] = jnp.zeros(agrad.shape, low)
+    agrad[0:SENT_ROWS, :] = residual_grad.astype(low)
+    mgrad[...] = contract(agrad[...], wp[...], 1, 1).astype(low)
+
+    def grad_rows(part, j):
+        return pl.ds(pl.multiple_of(part * width + peers[j] * PIECE, 16), PIECE)
+
+    def kept_rows(part, i):
+        return pl.ds((i * 4 + part) * PIECE, PIECE)
+
+    def come_rows(part, i):
+        return pl.ds((16 + i * 4 + part) * PIECE, PIECE)
+
+    def share(part):
+        return [
+            send(work.at[grad_rows(part, 2 * i + 1)], og.at[kept_rows(part, i)], 1)
+            for i in range(4)
+        ]
+
+    def gather_share(part, copies):
+        sent = []
+        for i in range(4):
+            copies[i].wait_recv()
+            rows = kept_rows(part, i)
+            og[rows, :] = (
+                work[grad_rows(part, 2 * i), :].astype(wide) + og[rows, :].astype(wide)
+            ).astype(low)
+            if i > 0:
+                sent.append(send(og.at[rows], og.at[come_rows(part, i - 1)], 2 * i))
+        return sent
+
+    def total_share(part, copies):
+        total = og[kept_rows(part, 0), :].astype(wide)
+        for i in range(3):
+            copies[i].wait_recv()
+            total = total + og[come_rows(part, i), :].astype(wide)
+        grad_attn[pl.ds(part * PIECE, PIECE), :] = total.astype(low)
+
+    def attend_back(p, carry):
+        queries = tri[:, head_columns(p, 0)]
+        key_rows = tri[:, head_columns(p, 1)]
+        value_rows = tri[:, head_columns(p, 2)]
+        mixed = mgrad[:, head_columns(p, 0)]
+        results = []
+        for side in range(2):
+            weights = probs[2 * p + side]
+            value_grad = contract(weights.astype(low), mixed, 0, 0)
+            weight_grad = contract(one_head(mixed, side), value_rows, 1, 1)
+            score_grad = (
+                weights
+                * (weight_grad - jnp.sum(weights * weight_grad, axis=-1, keepdims=True))
+                * score_scale
+            ).astype(low)
+            query_grad = jnp.dot(score_grad, key_rows, preferred_element_type=wide)
+            key_grad = contract(score_grad, queries, 0, 0)
+            results.append((query_grad, key_grad, value_grad))
+        for third in range(3):
+            tri[:, head_columns(p, third)] = jnp.where(
+                lane < 64, results[0][third], results[1][third]
+            ).astype(low)
+        return carry
+
+    out_copies[1].cross()
+    out_copies[0].fall()
+    work[3 * width : 4 * width, :] = contract(heads[...], agrad[...], 0, 0).astype(low)
+    share_p = share(3)
+    lax.fori_loop(0, 3, attend_back, 0)
+    out_copies[2].cross()
+    out_copies[1].fall()
+    lax.fori_loop(3, 6, attend_back, 0)
+    out_copies[2].fall()
+    grad_in_local.wait()
+    for copy in grad_in_copies:
+        copy.wait_recv()
+    for e in range(experts):
+        in_copies[e].rise()
+
+    def weight_grad_of(part):
+        work[part * width : (part + 1) * width, :] = contract(
+            ln_a[...], tri[:, part * width : (part + 1) * width], 0, 0
+        ).astype(low)
+
+    weight_grad_of(2)
+    share_v = share(2)
+    come_p = gather_share(3, share_p)
+    weight_grad_of(1)
+    share_k = share(1)
+    come_v = gather_share(2, share_v)
+    weight_grad_of(0)
+    share_q = share(0)
+    come_k = gather_share(1, share_k)
+    ln_grad = contract(tri[0:SENT_ROWS, :], wq[...], 1, 1)
+    come_q = gather_share(0, share_q)
+    normed = normed_a[0:SENT_ROWS, :]
+    gain_a_grad = jnp.sum(ln_grad * normed, axis=0, keepdims=True)
+    shift_a_grad = jnp.sum(ln_grad, axis=0, keepdims=True)
+    row16 = lax.broadcasted_iota(jnp.int32, (16, width), 0)
+    small = jnp.where(row16 < experts, route_grad[...], 0.0)
+    for row, value in (
+        (3, gain_a_grad),
+        (4, shift_a_grad),
+        (5, gain_m_grad),
+        (6, shift_m_grad),
+    ):
+        small = small + jnp.where(row16 == row, value, 0.0)
+    small_grad[0] = small.astype(low)
+    swap = send(small_grad.at[0], small_swap.at[0], 1)
+    igrad_ref[...] = (
+        res_grad[...] + norm_back(ln_grad * gain_first, normed, inv_a[0:SENT_ROWS, :])
+    ).astype(low)
+    in_copies[0].cross()
+    for step in range(2):
+        swap.wait_recv()
+        small_grad[step + 1] = (
+            small_grad[step].astype(wide) + small_swap[step].astype(wide)
+        ).astype(low)
+        swap = send(small_grad.at[step + 1], small_swap.at[step + 1], 2 << step)
+    in_copies[1].cross()
+    in_copies[0].fall()
+    total_share(3, come_p)
+    total_share(2, come_v)
+    in_copies[2].cross()
+    in_copies[1].fall()
+    total_share(1, come_k)
+    total_share(0, come_q)
+    swap.wait_recv()
+    grad_attn[4 * PIECE : 4 * PIECE + 16, :] = (
+        small_grad[2].astype(wide) + small_swap[2].astype(wide)
+    ).astype(low)
+    attn_copies.rise()
+    output = resid[0:SENT_ROWS, :] + sr_out[0:SENT_ROWS, :].astype(wide)
+    for i in range(3):
+        out_sends[i].wait_recv()
+        output = output + rr_out[i].astype(wide)
+    out_ref[...] = output.astype(low)
+    in_copies[2].fall()
+    attn_copies.cross()
+    attn_copies.fall()
+    for copies in out_copies + in_copies + [attn_copies]:
+        copies.finish()
+    for copy in unsent:
+        if id(copy) not in settled:
+            copy.wait_send()
+def grouped(
+    tokens,
+    cotangent,
+    expert_index,
+    slot_index,
+    kept_mask,
+    gain_attn,
+    shift_attn,
+    w_qkv,
+    w_proj,
+    gain_moe,
+    shift_moe,
+    w_router,
+    w_in,
+    w_out,
+):
+    low = jnp.bfloat16
+    wide = jnp.float32
+    rows, width = tokens.shape
+    owned, experts, hidden = w_in.shape
+    part = w_out.shape[0]
+    shard = lax.axis_index("shard")
+    tokens_in = jnp.pad(tokens, ((0, TILE_ROWS - rows), (0, 0)))
+    placed = kept_mask == 1
+    choice = jnp.pad(
+        jnp.where(placed, expert_index, experts), ((0, 256 - rows), (0, 0)), constant_values=experts
+    )
+    slot = jnp.pad(jnp.where(placed, slot_index, 0), ((0, 256 - rows), (0, 0)))
+    table = jnp.concatenate([choice, slot], axis=0).T.astype(low)
+    table = jnp.pad(table, ((TABLE_ROW - rows, SENT_ROWS - TABLE_ROW - 2), (0, width - 512)))
+    message = jnp.concatenate([cotangent, table], axis=0)
+    small = jnp.concatenate(
+        [w_router.T, jnp.stack([gain_attn, shift_attn, gain_moe, shift_moe])], axis=0
+    ).astype(low)
+    small = lax.dynamic_update_slice(
+        jnp.zeros((16, width), low), small, (jnp.int32(0), shard * owned)
+    )
+    inner = jnp.transpose(w_in, (1, 0, 2)).astype(low)
+    outer = jnp.transpose(w_out, (1, 0, 2)).astype(low)
+    slots = experts * CAP
+    total_slots = 8 * slots
+    vmem = pltpu.VMEM
+    token_shape = jax.ShapeDtypeStruct((SENT_ROWS, width), low)
+    attn_rows = 4 * PIECE + 16
+    scratch = [
+        vmem((8, 16, width), low),
+        vmem((16, width), wide),
+        vmem((width, 3 * width), low),
+        vmem((width, width), low),
+        vmem((experts, width, part), low),
+        vmem((TILE_ROWS, width), wide),
+        vmem((TILE_ROWS, 1), wide),
+        vmem((TILE_ROWS, width), low),
+        vmem((TILE_ROWS, 3 * width), low),
+        vmem((HEADS, TILE_ROWS, TILE_ROWS), wide),
+        vmem((TILE_ROWS, width), low),
+        vmem((TILE_ROWS, width), wide),
+        vmem((TILE_ROWS, 1), wide),
+        vmem((TILE_ROWS, 1), wide),
+        vmem((16 * TILE_ROWS, width), low),
+        vmem((8, slots, TILE_ROWS), low),
+        vmem((4 * width, width), low),
+        vmem((total_slots, width), low),
+        vmem((total_slots, 16), wide),
+        vmem((experts, 8 * CAP, part), low),
+        vmem((experts, 8 * CAP, part), low),
+        vmem((16, width), wide),
+        vmem((4, SENT_ROWS, width), low),
+        vmem((4, SENT_ROWS, width), low),
+        vmem((3, SENT_ROWS, width), low),
+        vmem((4 * SENT_ROWS, width), low),
+        vmem((3, SENT_ROWS, width), low),
+        vmem((experts, width, part), low),
+        vmem((experts, owned, hidden), low),
+        vmem((experts, part, width), low),
+        vmem((attn_rows, width), low),
+        vmem((experts, owned, hidden), low),
+        vmem((experts, part, width), low),
+        vmem((attn_rows, width), low),
+        vmem((experts, owned, hidden), low),
+        vmem((experts, part, width), low),
+        vmem((attn_rows, width), low),
+        vmem((SENT_ROWS, width), wide),
+        vmem((TILE_ROWS, width), low),
+        vmem((TILE_ROWS, width), low),
+        vmem((3, 16, width), low),
+        vmem((3, 16, width), low),
+        pltpu.SemaphoreType.DMA((160,)),
+        pltpu.SemaphoreType.DMA((160,)),
+        pltpu.SemaphoreType.DMA((16,)),
+    ]
+    inside = pl.BlockSpec(memory_space=vmem)
+    outside = pl.BlockSpec(memory_space=pl.ANY)
+    output, input_grad, outer_sum, inner_sum, attn_sum = pl.pallas_call(
+        mega,
+        out_shape=(
+            token_shape,
+            token_shape,
+            jax.ShapeDtypeStruct((experts, part, width), low),
+            jax.ShapeDtypeStruct((experts, owned, hidden), low),
+            jax.ShapeDtypeStruct((attn_rows, width), low),
+        ),
+        in_specs=[inside, inside, inside, inside, inside, outside, inside],
+        out_specs=(inside, inside, outside, outside, outside),
+        scratch_shapes=scratch,
+        compiler_params=pltpu.CompilerParams(
+            collective_id=0, has_side_effects=True, vmem_limit_bytes=VMEM_BYTES
+        ),
+    )(tokens_in, message, small, w_qkv, w_proj, inner, outer)
+    attn_grads = attn_sum[: 4 * owned].astype(wide).reshape(4, owned, width)
+    small_sum = lax.dynamic_slice(
+        attn_sum, (jnp.int32(4 * owned), shard * owned), (16, owned)
+    ).astype(wide)
+    return (
+        output[:rows],
+        input_grad[:rows],
+        small_sum[3],
+        small_sum[4],
+        jnp.concatenate([attn_grads[0], attn_grads[1], attn_grads[2]], axis=1),
+        attn_grads[3],
+        small_sum[5],
+        small_sum[6],
+        small_sum[:experts].T,
+        jnp.transpose(inner_sum, (1, 0, 2)).astype(wide),
+        jnp.transpose(outer_sum, (1, 0, 2)).astype(wide),
+    )
+
+
 def solution(mesh):
+    sizes = (mesh.shape["shard"], mesh.shape["rep"])
     return jax.shard_map(
-        shards,
+        grouped if sizes == (8, 4) else shards,
         mesh=mesh,
         in_specs=(
             P(("shard", "rep"), None),

time: 568 us -> 260 us (0.46)
  waiting for transfers between devices: 242 us -> 0 us
  Pallas kernels: 0 us -> 234 us
  blocking collectives: 133 us -> 0 us
  matrix products: 78.5 us -> 0 us
  local copies, waits for them, and re-layouts: 59.6 us -> 7.45 us
  between operations: 15.9 us -> 0.7 us
  starting transfers between devices: 14.4 us -> 0 us
    pallas_call x0 -> x1, Pallas kernels: none -> 234 us  [grouped(): pl.pallas_call(mega, out_shape=(token_shape, token_shape, jax.ShapeDtypeS...]
    psum x1 -> x0, waiting for transfers between devices: 157 us -> none  [shards(): outer_owned = lax.psum(outer_wgrad.astype(low), 'rep').astype(wide)]
    unnamed x2 -> x0, blocking collectives: 75.8 us -> none
    dot_general x23 -> x0, matrix products: 73.5 us -> none  [the longest x2 9.36 us: to_slots(): jnp.einsum('bst,btd->bsd', placed_low, values, preferred_element_type=wide)]
    all_gather x2 -> x0, blocking collectives: 57.2 us -> none  [gathered(): return lax.all_gather(value, 'shard', axis=0, tiled=True)]
    all_gather x4 -> x0, waiting for transfers between devices: 41.5 us -> none  [gathered(): return lax.all_gather(value, 'shard', axis=0, tiled=True)]
    all_to_all x2 -> x0, waiting for transfers between devices: 27.2 us -> none  [the longest x1 27.2 us: shards(): lax.all_to_all(inner_wgrad.astype(low).reshape(group, -1, experts, inner_...]
    reduce_scatter x1 -> x0, waiting for transfers between devices: 15.8 us -> none  [scattered(): return lax.psum_scatter(values, 'shard', scatter_dimension=0, tiled=True)]
  transfers between devices with their start and end apart: 10 -> 0, of which waited for: 5 -> 0; matrix products, arithmetic and copies ran while one was open for 14% -> 0% of each run, Pallas kernels for 0% -> 0%
where the time goes in v2:
time: 260 us; the launch traced here: 259 us
  Pallas kernels  234 us (90%)
  other arithmetic  16.6 us (6%)
  local copies, waits for them, and re-layouts  7.45 us (3%)
    pallas_call x1, Pallas kernels, grouped(): pl.pallas_call(mega, out_shape=(token_shape, token_shape, jax.ShapeDtypeS...  234 us

profile of v2, /device:TPU:0, one launch (start us, length us, event | category | flops | bytes accessed | tf_op | source)
XLA Modules:
  0.0 259.1 jit_solution(8679615175283614366)
XLA Ops:
  0.6 0.7 convert_bitcast_fusion.4
  1.3 0.7 convert_bitcast_fusion.7
  2.0 0.7 convert_bitcast_fusion.5
  2.7 0.7 select_convert_fusion.1
  3.5 0.3 dynamic_update_slice.3.small_ref
  3.8 0.0 copy-start.3
  3.8 1.7 fusion.1.ups_ref
  5.5 1.7 pad.17.tok_ref
  7.3 0.0 copy-start
  7.3 3.6 %convert_bitcast_fusion.3.inner_hbm = bf16[3,96,3072]{2,1,0:T(8,128)(2,1)} fusion(f32[96,3,3072]{2,0,1:T(8,128)} %param.26), kind=kLoop, calls=%fused_computation.3 | loop fusion | flops 884736 | bytes 5308416 | tf_op jit(solution)/shard_map/convert_element_type | solution.py:966
  10.9 0.0 copy-done.3
  10.9 0.0 copy-done
  10.9 1.4 convert_bitcast_fusion.2.outer_ref
  12.2 234.3 %shard_map.221 = (bf16[208,768]{1,0:T(8,128)(2,1)}, bf16[208,768]{1,0:T(8,128)(2,1)}, bf16[3,384,768]{2,1,0:T(8,128)(2,1)}, bf16[3,96,3072]{2,1,0:T(8,128)(2,1)}, bf16[400,768]{1,0:T(8,128)(2,1)}) custom-call(bf16[256,768]{1,0:T(8,128)(2,1)} %pad.17.tok_ref, bf16[208,768]{1,0:T(8,128)(2,1)} %fusion.1.ups_ref, bf16[16,768]{1,0:T(8,128)(2,1)} %copy-done.3, ...), custom_call_target="tpu_custom_call" | custom-call | tf_op jit(solution)/shard_map/pallas_call | solution.py:1022
  246.6 1.7 slice.40
  248.3 0.8 dynamic-slice_convert_fusion
  249.1 0.6 slice_bitcast_fusion
  249.6 0.5 slice_bitcast_fusion.1
  250.2 1.7 slice.41
  251.9 1.1 slice_convert_fusion
  253.0 0.0 copy-start.2
  253.0 0.8 fusion.4
  253.8 1.0 pad_maximum_fusion
  254.8 0.0 copy-done.2
  254.8 0.0 copy-start.1
  254.8 2.2 convert_bitcast_fusion.1
  257.0 0.0 copy-done.1
  257.0 2.1 convert_bitcast_fusion
  (3 shorter events, 0.0 us)
Async XLA Ops:
  3.8 7.1 %copy-start.3 = (bf16[16,768]{1,0:T(8,128)(2,1)}, bf16[16,768]{1,0:T(8,128)(2,1)S(1)}, u32[]{:S(2)}) copy-start(bf16[16,768]{1,0:T(8,128)(2,1)S(1)} %dynamic_update_slice.3.small_ref) | copy-start | bytes 73732
  7.3 3.6 %copy-start = (f32[384,3,768]{2,0,1:T(8,128)S(1)}, f32[384,3,768]{2,0,1:T(8,128)}, u32[]{:S(2)}) copy-start(f32[384,3,768]{2,0,1:T(8,128)} %param.27) | copy-start | bytes 10616836
  253.0 1.8 copy-start.2
  254.8 2.2 copy-start.1

commit v3 on v2

--- a/solution.py
+++ b/solution.py
@@ -250,15 +250,25 @@
 
 TILE_ROWS = 256
 SENT_ROWS = 208
-TABLE_ROW = 200
+CUTS = 4
+Z_STEP = 3.2
+Z_LAG = 1.5
+DEPTH = 3
 PIECE = 96
 NEGATIVE = -1e30
 
 
 def mega(
     tok_ref,
-    ups_ref,
-    small_ref,
+    cot_ref,
+    expert_ref,
+    slot_ref,
+    kept_ref,
+    gain_a_ref,
+    shift_a_ref,
+    gain_m_ref,
+    shift_m_ref,
+    router_ref,
     qkv_ref,
     proj_ref,
     inner_hbm,
@@ -268,6 +278,10 @@
     go_hbm,
     gi_hbm,
     ga_hbm,
+    piece_ref,
+    stage,
+    piece,
+    table_buf,
     smalls,
     small_sum,
     wq,
@@ -369,7 +383,7 @@
         )
 
     def send(src, dst, j):
-        copy = describe(src, dst, (peers[j], rep))
+        copy = describe(src, dst, (peers[j], rep) if j < 8 else (shard, pair))
         copy.start()
         unsent.append(copy)
         return copy
@@ -436,33 +450,66 @@
 
     own_rows = pl.ds(off(shard, PIECE), PIECE)
     small_copies = []
-    smalls[0] = small_ref[...]
+    staged = local(inner_hbm.at[0], stage)
+    experts = router_ref.shape[0]
+    piece[...] = jnp.zeros(piece.shape, wide)
+    piece[0:experts, 0:PIECE] = router_ref[...]
+    for row, ref in enumerate((gain_a_ref, shift_a_ref, gain_m_ref, shift_m_ref)):
+        piece[experts + row : experts + row + 1, 0:PIECE] = ref[...]
+    own_at = lax.broadcasted_iota(jnp.int32, (128, width), 0)
+    own_to = lax.broadcasted_iota(jnp.int32, (128, width), 1) - shard * PIECE
+    own_pick = jnp.where(jnp.logical_and(own_at == own_to, own_at < PIECE), 1.0, 0.0).astype(low)
+    kept = kept_ref[...] == 1
+    table_buf[...] = jnp.zeros(table_buf.shape, wide)
+    table_buf[8:10, 0:256] = jnp.full((2, 256), experts, wide)
+    table_buf[8:10, 0:SEQ] = jnp.where(kept, expert_ref[...], experts).astype(wide)
+    table_buf[8:10, 256 : 256 + SEQ] = jnp.where(kept, slot_ref[...], 0).astype(wide)
+    smalls[0] = (
+        jnp.dot(piece[...].astype(low), own_pick, preferred_element_type=wide) + table_buf[...]
+    ).astype(low)
     for j in range(1, 8):
         small_copies.append(send(smalls.at[0], smalls.at[j], j))
     wq[own_rows, :] = qkv_ref[...].astype(low)
     gather_q = Gather(weight_view(wq), (0, 48), (48, 48))
     gather_q.begin()
     wp[own_rows, :] = proj_ref[...].astype(low)
-    rows_buf[ups_base : ups_base + SENT_ROWS, :] = ups_ref[...]
-    inputs = tok_ref[...].astype(wide)
+    res_grad[192:SENT_ROWS, :] = jnp.zeros((SENT_ROWS - 192, width), wide)
+    res_grad[0:SEQ, :] = cot_ref[...].astype(wide)
+    rows_buf[ups_base : ups_base + SENT_ROWS, :] = res_grad[...].astype(low)
+    resid[192:TILE_ROWS, :] = jnp.zeros((TILE_ROWS - 192, width), wide)
+    resid[0:SEQ, :] = tok_ref[...].astype(wide)
+    inputs = resid[...]
     normed, inverse = normalize(inputs)
     normed_a[...] = normed
     inv_a[...] = inverse
+
+    def inner_cast(e):
+        for d in range(8):
+            grad_in[e, d * PIECE : (d + 1) * PIECE, :] = stage[
+                :, d * part : (d + 1) * part
+            ].astype(low)
+
+    part = win.shape[2]
+    for e in range(experts):
+        staged.wait()
+        inner_cast(e)
+        if e < experts - 1:
+            staged = local(inner_hbm.at[e + 1], stage)
     gather_q.pass_on()
-    gather_p = Gather(weight_view(wp), (0, 48), (48, 48))
-    gather_p.begin()
-    part = win.shape[2]
-    inner_copies = [
-        send(
-            inner_hbm.at[:, :, pl.ds(off(peers[j], part), part)],
-            win.at[:, own_rows, :],
-            j,
-        )
-        for j in range(1, 8)
-    ]
-    inner_own = local(inner_hbm.at[:, :, pl.ds(off(shard, part), part)], win.at[:, own_rows, :])
-    gather_u = Gather(row_view(ups_base), (0, 112), (112, 96))
-    gather_u.begin()
+    half_at = (rep % 2) * (PIECE // 2)
+
+    def inner_half(j):
+        return pl.ds(pl.multiple_of(peers[j] * PIECE + half_at, 16), PIECE // 2)
+
+    inner_own = local(grad_in.at[:, own_rows, :], win.at[:, own_rows, :])
+    inner_passed = []
+
+    def inner_pass(numbers):
+        for j in numbers:
+            inner_copies[j].wait_recv()
+            rows = win.at[:, inner_half(j), :]
+            inner_passed.append(send(rows, rows, 8))
+
     for copy in small_copies:
         copy.wait_recv()
     total = smalls[0].astype(wide)
@@ -472,7 +519,21 @@
     gain_first, shift_first = small_sum[3:4, :], small_sum[4:5, :]
     gain_second, shift_second = small_sum[5:6, :], small_sum[6:7, :]
     ln_a[...] = (normed_a[...] * gain_first + shift_first).astype(low)
+    slots = onehot.shape[1]
+    slot_at = lax.broadcasted_iota(jnp.int32, (slots, TILE_ROWS), 0).astype(wide)
+
+    def route_step(j, carry):
+        table = smalls[j].astype(wide)
+        first = table[8:9, 0:256] * CAP + table[8:9, 256:512]
+        second = table[9:10, 0:256] * CAP + table[9:10, 256:512]
+        hit = jnp.logical_or(slot_at == first, slot_at == second)
+        onehot[j] = jnp.where(hit, 1.0, 0.0).astype(low)
+        return carry
+
+    lax.fori_loop(0, 8, route_step, 0)
     gather_q.last()
+    gather_p = Gather(weight_view(wp), (0, 48), (48, 48))
+    gather_p.begin()
     for copy in gather_q.from_s:
         copy.wait_recv()
 
@@ -484,6 +545,15 @@
         return carry
 
     lax.fori_loop(0, 6, triple_step, 0)
+    gather_p.pass_on()
+    inner_copies = {
+        j: send(
+            grad_in.at[:, inner_half(j), :],
+            win.at[:, inner_half(0), :],
+            j,
+        )
+        for j in range(1, 8)
+    }
 
     lane = lax.broadcasted_iota(jnp.int32, (TILE_ROWS, 128), 1)
     key_at = lax.broadcasted_iota(jnp.int32, (TILE_ROWS, TILE_ROWS), 1)
@@ -512,14 +582,11 @@
         heads[:, head_columns(p, 0)] = jnp.where(lane < 64, mixed[0], mixed[1]).astype(low)
         return carry
 
-    lax.fori_loop(0, 3, attend, 0)
-    gather_p.pass_on()
-    lax.fori_loop(3, 6, attend, 0)
-    gather_u.pass_on()
+    lax.fori_loop(0, 6, attend, 0)
     gather_p.last()
     for copy in gather_p.from_s:
         copy.wait_recv()
-    residual = tok_ref[...].astype(wide) + jnp.dot(
+    residual = resid[...] + jnp.dot(
         heads[...], wp[...], preferred_element_type=wide
     )
     resid[...] = residual
@@ -530,28 +597,11 @@
     rows_buf[0:SENT_ROWS, :] = ln_two[0:SENT_ROWS, :]
     gather_l = Gather(row_view(0), (0, 112), (112, 96))
     gather_l.begin()
-    gather_u.last()
-    for copy in gather_u.from_s:
-        copy.wait_recv()
-
-    slots = onehot.shape[1]
-    slot_at = lax.broadcasted_iota(jnp.int32, (slots, TILE_ROWS), 0).astype(wide)
-
-    def route_step(j, carry):
-        start = pl.multiple_of(ups_base + j * TILE_ROWS + 192, 16)
-        table = rows_buf[pl.ds(start, 16), :].astype(wide)
-        first = table[8:9, 0:256] * CAP + table[8:9, 256:512]
-        second = table[9:10, 0:256] * CAP + table[9:10, 256:512]
-        hit = jnp.logical_or(slot_at == first, slot_at == second)
-        onehot[j] = jnp.where(hit, 1.0, 0.0).astype(low)
-        return carry
-
-    lax.fori_loop(0, 8, route_step, 0)
+    inner_pass((1, 2, 3, 4, 5, 6, 7))
     router = small_sum[...].astype(low)
     lane16 = lax.broadcasted_iota(jnp.int32, (slots, 16), 1)
     expert_of = lax.broadcasted_iota(jnp.int32, (slots, 16), 0)
     own_lane = jnp.logical_and(expert_of >= lane16 * CAP, expert_of < lane16 * CAP + CAP)
-    experts = win.shape[0]
 
     def expert_rows(e, j, blocks=1):
         return pl.ds(pl.multiple_of((e * 8 + j) * CAP, 16), blocks * CAP)
@@ -559,19 +609,24 @@
     def dispatch_step(j, carry):
         picks = onehot[j]
         ln_rows = rows_buf[pl.ds(off(j, TILE_ROWS), TILE_ROWS), :]
-        up_rows = rows_buf[pl.ds(pl.multiple_of(ups_base + j * TILE_ROWS, 16), TILE_ROWS), :]
         sent = jnp.dot(picks, ln_rows, preferred_element_type=wide).astype(low)
         logits = jnp.where(lane16 < experts, contract(sent, router, 1, 1), NEGATIVE)
         powers = jnp.exp(logits - jnp.max(logits, axis=-1, keepdims=True))
         chances = powers / jnp.sum(powers, axis=-1, keepdims=True)
-        gate = jnp.sum(jnp.where(own_lane, chances, 0.0), axis=-1, keepdims=True)
-        ups = jnp.dot(picks, up_rows, preferred_element_type=wide)
-        upward = (ups * gate).astype(low)
         for e in range(experts):
             rows = expert_rows(e, j)
             work[rows, :] = sent[e * CAP : (e + 1) * CAP]
-            og[rows, :] = upward[e * CAP : (e + 1) * CAP]
             route[rows, :] = chances[e * CAP : (e + 1) * CAP]
+        return carry
+
+    def upward_step(j, carry):
+        up_rows = rows_buf[pl.ds(pl.multiple_of(ups_base + j * TILE_ROWS, 16), TILE_ROWS), :]
+        ups = jnp.dot(onehot[j], up_rows, preferred_element_type=wide)
+        chances = jnp.concatenate([route[expert_rows(e, j), :] for e in range(experts)], axis=0)
+        gate = jnp.sum(jnp.where(own_lane, chances, 0.0), axis=-1, keepdims=True)
+        upward = (ups * gate).astype(low)
+        for e in range(experts):
+            og[expert_rows(e, j), :] = upward[e * CAP : (e + 1) * CAP]
         return carry
 
     def hidden_step(g):
@@ -593,18 +648,31 @@
 
         lax.fori_loop(0, experts, step, 0)
 
-    inner_own.wait()
-    for copy in inner_copies:
-        copy.wait_recv()
     gather_l.pass_on()
+    gather_u = Gather(row_view(ups_base), (0, 112), (112, 96))
+    gather_u.begin()
     gather_l.from_s[0].wait_recv()
     lax.fori_loop(0, 2, dispatch_step, 0)
-    hidden_step(0)
     gather_l.last()
-    for g in range(1, 4):
+    for g in range(1, 3):
         gather_l.from_s[g].wait_recv()
         lax.fori_loop(2 * g, 2 * g + 2, dispatch_step, 0)
-        hidden_step(g)
+    inner_own.wait()
+    for copy in inner_passed:
+        copy.wait_recv()
+    hidden_step(0)
+    gather_u.pass_on()
+    hidden_step(1)
+    hidden_step(2)
+    gather_l.from_s[3].wait_recv()
+    lax.fori_loop(6, 8, dispatch_step, 0)
+    gather_u.last()
+    hidden_step(3)
+    for copy in gather_u.from_s:
+        copy.wait_recv()
+    lax.fori_loop(0, 8, upward_step, 0)
+
+    ready, raised, left = [], [], []
 
     class Copies:
         def __init__(self, own, mid, end, out, rows):
@@ -612,6 +680,8 @@
             self.up = describe(own, end, (shard, pair))
             self.over = describe(own, mid, (shard, across))
             self.down = describe(end, end, (shard, pair))
+            self.write = pltpu.make_async_copy(end, out, local_sems.at[local_count[0]])
+            local_count[0] += 1
 
         def add(self, target, other):
             size = self.rows
@@ -626,57 +696,108 @@
             lax.fori_loop(0, target.shape[0] // size, step, 0)
 
         def rise(self):
-            @pl.when(is_end)
-            def _():
-                self.up.start()
+            ready.append(self)
+            pump()
 
         def cross(self):
+            self.up.wait_recv()
+            self.add(self.own, self.end)
+            self.over.start()
+
+        def fall(self):
+            self.over.wait_recv()
+            self.add(self.end, self.mid)
+            self.down.start()
+            self.write.start()
+
+    out_cut, in_cut = part // CUTS, grad_in_own.shape[2] // CUTS
+    out_copies = [
+        Copies(
+            *(
+                ref.at[e, pl.ds(h * out_cut, out_cut)]
+                for ref in (grad_out, mid_out, end_out, go_hbm)
+            ),
+            48,
+        )
+        for e in range(experts)
+        for h in range(CUTS)
+    ]
+    in_copies = [
+        Copies(
+            *(
+                ref.at[e, :, pl.ds(h * in_cut, in_cut)]
+                for ref in (grad_in_own, mid_in, end_in, gi_hbm)
+            ),
+            48,
+        )
+        for e in range(experts)
+        for h in range(CUTS)
+    ]
+    attn_copies = {
+        p: Copies(
+            *(ref.at[pl.ds(p * PIECE, size)] for ref in (grad_attn, mid_attn, end_attn, ga_hbm)),
+            size // 2 if size > 16 else size,
+        )
+        for p, size in ((3, PIECE), (2, PIECE), (1, PIECE), (0, PIECE), (4, 16))
+    }
+    all_copies = out_copies + in_copies + list(attn_copies.values())
+
+    def pump():
+        @pl.when(is_end)
+        def _():
+            while len(raised) < len(ready) and len(raised) < len(left) + DEPTH:
+                ready[len(raised)].up.start()
+                raised.append(1)
+
+    plan = []
+    moment = 0.0
+    for number, copies in enumerate(all_copies):
+        span = Z_STEP if number < 2 * experts * CUTS else 3.2
+        moment += span
+        plan.append((moment + span + Z_LAG, 0, copies))
+        plan.append((moment + 3 * span + 2 * Z_LAG, 1, copies))
+    plan.sort(key=lambda step: step[:2])
+
+    def tend(until):
+        steps = []
+        while plan and plan[0][0] <= until:
+            steps.append(plan.pop(0))
+        for _, kind, copies in steps:
+            if kind == 0:
+                assert len(raised) > len(left)
+
             @pl.when(is_mid)
             def _():
-                self.up.wait_recv()
-                self.add(self.own, self.end)
-                self.over.start()
-
-        def fall(self):
-            @pl.when(is_mid)
-            def _():
-                self.over.wait_recv()
-                self.add(self.end, self.mid)
-                self.down.start()
-
-        def finish(self):
-            @pl.when(is_end)
-            def _():
-                self.up.wait_send()
-                self.down.wait_recv()
-
-            write = local(self.end, self.out)
-
-            @pl.when(is_mid)
-            def _():
-                self.over.wait_send()
-                self.down.wait_send()
-
-            write.wait()
-
-    out_copies = [
-        Copies(grad_out.at[e], mid_out.at[e], end_out.at[e], go_hbm.at[e], 64) for e in range(experts)
-    ]
-    in_copies = [
-        Copies(grad_in_own.at[e], mid_in.at[e], end_in.at[e], gi_hbm.at[e], 16)
-        for e in range(experts)
-    ]
-    attn_copies = Copies(grad_attn, mid_attn, end_attn, ga_hbm, 80)
+                (copies.fall if kind else copies.cross)()
+
+            if kind == 0:
+
+                @pl.when(is_end)
+                def _():
+                    copies.up.wait_send()
+
+                left.append(1)
+                pump()
 
     for e in range(experts):
         grad_out[e] = contract(act[e], og[expert_rows(e, 0, 8), :], 0, 0).astype(low)
-        out_copies[e].rise()
+        for h in range(CUTS):
+            out_copies[CUTS * e + h].rise()
 
     settle(gather_l.all)
+    settle(inner_copies.values())
     settle(gather_u.all)
     route_grad[...] = jnp.zeros(route_grad.shape, wide)
     half = act.shape[1] // 2
     lane_h = lax.broadcasted_iota(jnp.int32, (half, 16), 1)
+
+    def inner_step(i, carry):
+        e = i // 2
+        rows = pl.ds(off(i % 2, half), half)
+        flat = pl.ds(pl.multiple_of(i * half, 16), half)
+        inner = contract(og[flat, :], outer_ref[e], 1, 1) * slope[e, rows, :].astype(wide)
+        slope[e, rows, :] = inner.astype(low)
+        return carry
 
     def back_step(i, carry):
         e = i // 2
@@ -690,16 +811,41 @@
         logit = (pull * (jnp.where(lane_h == e, 1.0, 0.0) - chances)).astype(low)
         logit = jnp.where(lane_h < experts, logit, jnp.zeros_like(logit))
         rows_buf[flat, :] = (gone * gate).astype(low)
-        inner = contract(upward, outer_ref[e], 1, 1) * slope[e, rows, :].astype(wide)
-        inner = inner.astype(low)
-        slope[e, rows, :] = inner
         og[flat, :] = (
-            contract(inner, win[e], 1, 1) + jnp.dot(logit, router, preferred_element_type=wide)
+            contract(slope[e, rows, :], win[e], 1, 1)
+            + jnp.dot(logit, router, preferred_element_type=wide)
         ).astype(low)
         route_grad[...] += contract(logit, work[flat, :], 0, 0)
         return carry
 
-    lax.fori_loop(0, 2 * experts, back_step, 0)
+    grad_in_copies = []
+
+    def grad_in_send(e):
+        target = grad_in_own.at[e, :, pl.ds(off(shard, part), part)]
+        grad_in_copies.append(
+            [
+                send(grad_in.at[e, pl.ds(off(peers[j], PIECE), PIECE), :], target, j)
+                for j in range(1, 8)
+            ]
+        )
+        grad_in_copies[e].append(local(grad_in.at[e, own_rows, :], target))
+
+    def grad_in_wait(e):
+        for copy in grad_in_copies[e][:7]:
+            copy.wait_recv()
+        grad_in_copies[e][7].wait()
+        for h in range(CUTS):
+            in_copies[CUTS * e + h].rise()
+
+    for e in range(experts):
+        lax.fori_loop(2 * e, 2 * e + 2, inner_step, 0)
+        grad_in[e] = contract(work[expert_rows(e, 0, 8), :], slope[e], 0, 0).astype(low)
+        if e < experts - 1:
+            grad_in_send(e)
+        tend(4 + 2 * e)
+    for e in range(experts):
+        lax.fori_loop(2 * e, 2 * e + 2, back_step, 0)
+        tend(10.5 + 2.3 * e)
 
     def combine_back(j):
         joined = jnp.concatenate([og[expert_rows(e, j), :] for e in range(experts)], axis=0)
@@ -719,31 +865,7 @@
 
     lax.fori_loop(0, 4, odd_back, 0)
     swap_back = send(st_back, sr_back, 1)
-
-    def inner_grad_step(e, carry):
-        grad_in[e] = contract(work[expert_rows(e, 0, 8), :], slope[e], 0, 0).astype(low)
-        return carry
-
-    lax.fori_loop(0, experts, inner_grad_step, 0)
-    swap_back.wait_recv()
-
-    def even_back(i, carry):
-        sr_back[i] = (combine_back(2 * i) + sr_back[i].astype(wide)).astype(low)
-        return carry
-
-    lax.fori_loop(0, 4, even_back, 0)
-    back_copies = [send(sr_back.at[i], rr_back.at[i - 1], 2 * i) for i in range(1, 4)]
-    grad_in_copies = [
-        send(
-            grad_in.at[:, pl.ds(off(peers[j], PIECE), PIECE), :],
-            grad_in_own.at[:, :, pl.ds(off(shard, part), part)],
-            j,
-        )
-        for j in range(1, 8)
-    ]
-    grad_in_local = local(
-        grad_in.at[:, own_rows, :], grad_in_own.at[:, :, pl.ds(off(shard, part), part)]
-    )
+    tend(17)
 
     def odd_out(i, carry):
         rows = pl.ds(pl.multiple_of(stage_out + i * SENT_ROWS, 16), SENT_ROWS)
@@ -751,8 +873,17 @@
         return carry
 
     lax.fori_loop(0, 4, odd_out, 0)
+    tend(19)
+    swap_back.wait_recv()
+
+    def even_back(i, carry):
+        sr_back[i] = (combine_back(2 * i) + sr_back[i].astype(wide)).astype(low)
+        return carry
+
+    lax.fori_loop(0, 4, even_back, 0)
+    back_copies = [send(sr_back.at[i], rr_back.at[i - 1], 2 * i) for i in range(1, 4)]
     swap_out = send(rows_buf.at[pl.ds(stage_out, 4 * SENT_ROWS)], sr_out, 1)
-    out_copies[0].cross()
+    tend(22)
     swap_out.wait_recv()
 
     def even_out(i, carry):
@@ -761,24 +892,21 @@
         return carry
 
     lax.fori_loop(0, 4, even_out, 0)
+    tend(25)
+    for e in range(experts - 1):
+        grad_in_wait(e)
+    tend(38)
 
     for copy in back_copies:
         copy.wait_recv()
-    out_sends = [
-        send(sr_out.at[pl.ds(i * SENT_ROWS, SENT_ROWS)], rr_out.at[i - 1], 2 * i)
-        for i in range(1, 4)
-    ]
+    grad_in_send(experts - 1)
     ln_grad = sr_back[0].astype(wide)
     for i in range(3):
         ln_grad = ln_grad + rr_back[i].astype(wide)
     normed = (resid[0:SENT_ROWS, :] - mean_m[0:SENT_ROWS, :]) * inv_m[0:SENT_ROWS, :]
     gain_m_grad = jnp.sum(ln_grad * normed, axis=0, keepdims=True)
     shift_m_grad = jnp.sum(ln_grad, axis=0, keepdims=True)
-    upstream = jnp.where(
-        lax.broadcasted_iota(jnp.int32, (SENT_ROWS, width), 0) < SEQ,
-        ups_ref[...].astype(wide),
-        0.0,
-    )
+    upstream = res_grad[...]
     residual_grad = upstream + norm_back(
         ln_grad * gain_second, normed, inv_m[0:SENT_ROWS, :]
     )
@@ -820,6 +948,7 @@
             copies[i].wait_recv()
             total = total + og[come_rows(part, i), :].astype(wide)
         grad_attn[pl.ds(part * PIECE, PIECE), :] = total.astype(low)
+        attn_copies[part].rise()
 
     def attend_back(p, carry):
         queries = tri[:, head_columns(p, 0)]
@@ -845,20 +974,13 @@
             ).astype(low)
         return carry
 
-    out_copies[1].cross()
-    out_copies[0].fall()
     work[3 * width : 4 * width, :] = contract(heads[...], agrad[...], 0, 0).astype(low)
     share_p = share(3)
+    tend(43)
     lax.fori_loop(0, 3, attend_back, 0)
-    out_copies[2].cross()
-    out_copies[1].fall()
+    tend(46)
     lax.fori_loop(3, 6, attend_back, 0)
-    out_copies[2].fall()
-    grad_in_local.wait()
-    for copy in grad_in_copies:
-        copy.wait_recv()
-    for e in range(experts):
-        in_copies[e].rise()
+    tend(50)
 
     def weight_grad_of(part):
         work[part * width : (part + 1) * width, :] = contract(
@@ -874,6 +996,7 @@
     weight_grad_of(0)
     share_q = share(0)
     come_k = gather_share(1, share_k)
+    tend(54)
     ln_grad = contract(tri[0:SENT_ROWS, :], wq[...], 1, 1)
     come_q = gather_share(0, share_q)
     normed = normed_a[0:SENT_ROWS, :]
@@ -893,39 +1016,97 @@
     igrad_ref[...] = (
         res_grad[...] + norm_back(ln_grad * gain_first, normed, inv_a[0:SENT_ROWS, :])
     ).astype(low)
-    in_copies[0].cross()
+    grad_in_wait(experts - 1)
+    tend(57)
     for step in range(2):
         swap.wait_recv()
         small_grad[step + 1] = (
             small_grad[step].astype(wide) + small_swap[step].astype(wide)
         ).astype(low)
         swap = send(small_grad.at[step + 1], small_swap.at[step + 1], 2 << step)
-    in_copies[1].cross()
-    in_copies[0].fall()
+        tend(60 + 3 * step)
+    tend(72)
     total_share(3, come_p)
     total_share(2, come_v)
-    in_copies[2].cross()
-    in_copies[1].fall()
+    tend(76)
     total_share(1, come_k)
     total_share(0, come_q)
+    out_sends = [
+        send(sr_out.at[pl.ds(i * SENT_ROWS, SENT_ROWS)], rr_out.at[i - 1], 2 * i)
+        for i in range(1, 4)
+    ]
     swap.wait_recv()
     grad_attn[4 * PIECE : 4 * PIECE + 16, :] = (
         small_grad[2].astype(wide) + small_swap[2].astype(wide)
     ).astype(low)
-    attn_copies.rise()
+    attn_copies[4].rise()
+    tend(84)
     output = resid[0:SENT_ROWS, :] + sr_out[0:SENT_ROWS, :].astype(wide)
     for i in range(3):
         out_sends[i].wait_recv()
         output = output + rr_out[i].astype(wide)
     out_ref[...] = output.astype(low)
-    in_copies[2].fall()
-    attn_copies.cross()
-    attn_copies.fall()
-    for copies in out_copies + in_copies + [attn_copies]:
-        copies.finish()
+    tend(1000)
+    for copies in all_copies:
+
+        @pl.when(is_end)
+        def _():
+            copies.down.wait_recv()
+            copies.write.start()
+
+        @pl.when(is_mid)
+        def _():
+            copies.over.wait_send()
+            copies.down.wait_send()
+
+    for copies in all_copies:
+        copies.write.wait()
+    assert count[0] <= send_sems.shape[0] and local_count[0] <= local_sems.shape[0]
+    piece_ref[...] = contract(end_attn[4 * PIECE : 4 * PIECE + 16, :], own_pick, 1, 1)
     for copy in unsent:
         if id(copy) not in settled:
             copy.wait_send()
+
+
+def finish(
+    out_in,
+    igrad_in,
+    outer_in,
+    inner_in,
+    attn_in,
+    small_in,
+    out_ref,
+    igrad_ref,
+    outer_ref,
+    inner_ref,
+    qkv_ref,
+    proj_ref,
+    router_ref,
+    gain_a_ref,
+    shift_a_ref,
+    gain_m_ref,
+    shift_m_ref,
+):
+    wide = jnp.float32
+    outer_ref[...] = outer_in[...].astype(wide)
+    inner_ref[...] = inner_in[...].astype(wide)
+
+    @pl.when(pl.program_id(0) == 0)
+    def _():
+        rows, width = out_ref.shape
+        out_ref[...] = out_in[0:rows, :]
+        igrad_ref[...] = igrad_in[0:rows, :]
+        for third in range(3):
+            qkv_ref[:, third * width : (third + 1) * width] = attn_in[
+                third * PIECE : (third + 1) * PIECE, :
+            ].astype(wide)
+        proj_ref[...] = attn_in[3 * PIECE : 4 * PIECE, :].astype(wide)
+        experts = router_ref.shape[0]
+        router_ref[...] = small_in[0:experts, 0:PIECE]
+        for row, ref in enumerate((gain_a_ref, shift_a_ref, gain_m_ref, shift_m_ref)):
+            ref[...] = small_in[experts + row : experts + row + 1, 0:PIECE]
+
+
 def grouped(
     tokens,
     cotangent,
@@ -948,22 +1129,6 @@
     owned, experts, hidden = w_in.shape
     part = w_out.shape[0]
     shard = lax.axis_index("shard")
-    tokens_in = jnp.pad(tokens, ((0, TILE_ROWS - rows), (0, 0)))
-    placed = kept_mask == 1
-    choice = jnp.pad(
-        jnp.where(placed, expert_index, experts), ((0, 256 - rows), (0, 0)), constant_values=experts
-    )
-    slot = jnp.pad(jnp.where(placed, slot_index, 0), ((0, 256 - rows), (0, 0)))
-    table = jnp.concatenate([choice, slot], axis=0).T.astype(low)
-    table = jnp.pad(table, ((TABLE_ROW - rows, SENT_ROWS - TABLE_ROW - 2), (0, width - 512)))
-    message = jnp.concatenate([cotangent, table], axis=0)
-    small = jnp.concatenate(
-        [w_router.T, jnp.stack([gain_attn, shift_attn, gain_moe, shift_moe])], axis=0
-    ).astype(low)
-    small = lax.dynamic_update_slice(
-        jnp.zeros((16, width), low), small, (jnp.int32(0), shard * owned)
-    )
-    inner = jnp.transpose(w_in, (1, 0, 2)).astype(low)
     outer = jnp.transpose(w_out, (1, 0, 2)).astype(low)
     slots = experts * CAP
     total_slots = 8 * slots
@@ -971,6 +1136,9 @@
     token_shape = jax.ShapeDtypeStruct((SENT_ROWS, width), low)
     attn_rows = 4 * PIECE + 16
     scratch = [
+        vmem((owned, hidden), wide),
+        vmem((16, 128), wide),
+        vmem((16, width), wide),
         vmem((8, 16, width), low),
         vmem((16, width), wide),
         vmem((width, 3 * width), low),
@@ -1013,13 +1181,13 @@
         vmem((TILE_ROWS, width), low),
         vmem((3, 16, width), low),
         vmem((3, 16, width), low),
-        pltpu.SemaphoreType.DMA((160,)),
-        pltpu.SemaphoreType.DMA((160,)),
-        pltpu.SemaphoreType.DMA((16,)),
+        pltpu.SemaphoreType.DMA((256,)),
+        pltpu.SemaphoreType.DMA((256,)),
+        pltpu.SemaphoreType.DMA((48,)),
     ]
     inside = pl.BlockSpec(memory_space=vmem)
     outside = pl.BlockSpec(memory_space=pl.ANY)
-    output, input_grad, outer_sum, inner_sum, attn_sum = pl.pallas_call(
+    output, input_grad, outer_sum, inner_sum, attn_sum, small_sum = pl.pallas_call(
         mega,
         out_shape=(
             token_shape,
@@ -1027,30 +1195,82 @@
             jax.ShapeDtypeStruct((experts, part, width), low),
             jax.ShapeDtypeStruct((experts, owned, hidden), low),
             jax.ShapeDtypeStruct((attn_rows, width), low),
+            jax.ShapeDtypeStruct((16, 128), wide),
         ),
-        in_specs=[inside, inside, inside, inside, inside, outside, inside],
-        out_specs=(inside, inside, outside, outside, outside),
+        in_specs=[inside] * 12 + [outside, inside],
+        out_specs=(inside, inside, outside, outside, outside, inside),
         scratch_shapes=scratch,
         compiler_params=pltpu.CompilerParams(
             collective_id=0, has_side_effects=True, vmem_limit_bytes=VMEM_BYTES
         ),
-    )(tokens_in, message, small, w_qkv, w_proj, inner, outer)
-    attn_grads = attn_sum[: 4 * owned].astype(wide).reshape(4, owned, width)
-    small_sum = lax.dynamic_slice(
-        attn_sum, (jnp.int32(4 * owned), shard * owned), (16, owned)
-    ).astype(wide)
+    )(
+        tokens,
+        cotangent,
+        expert_index.T,
+        slot_index.T,
+        kept_mask.T,
+        gain_attn.reshape(1, owned),
+        shift_attn.reshape(1, owned),
+        gain_moe.reshape(1, owned),
+        shift_moe.reshape(1, owned),
+        w_router.T,
+        w_qkv,
+        w_proj,
+        jnp.transpose(w_in, (1, 0, 2)),
+        outer,
+    )
+
+    def whole(*shape):
+        return pl.BlockSpec(shape, lambda e: (0,) * len(shape))
+
+    def one(*shape):
+        return pl.BlockSpec((1, *shape), lambda e: (e, 0, 0))
+
+    finals = pl.pallas_call(
+        finish,
+        grid=(experts,),
+        out_shape=(
+            jax.ShapeDtypeStruct((rows, width), low),
+            jax.ShapeDtypeStruct((rows, width), low),
+            jax.ShapeDtypeStruct((experts, part, width), wide),
+            jax.ShapeDtypeStruct((experts, owned, hidden), wide),
+            jax.ShapeDtypeStruct((owned, 3 * width), wide),
+            jax.ShapeDtypeStruct((owned, width), wide),
+            jax.ShapeDtypeStruct((experts, owned), wide),
+        )
+        + (jax.ShapeDtypeStruct((1, owned), wide),) * 4,
+        in_specs=[
+            whole(SENT_ROWS, width),
+            whole(SENT_ROWS, width),
+            one(part, width),
+            one(owned, hidden),
+            whole(attn_rows, width),
+            whole(16, 128),
+        ],
+        out_specs=(
+            whole(rows, width),
+            whole(rows, width),
+            one(part, width),
+            one(owned, hidden),
+            whole(owned, 3 * width),
+            whole(owned, width),
+            whole(experts, owned),
+        )
+        + (whole(1, owned),) * 4,
+        compiler_params=pltpu.CompilerParams(vmem_limit_bytes=VMEM_BYTES // 2),
+    )(output, input_grad, outer_sum, inner_sum, attn_sum, small_sum)
     return (
-        output[:rows],
-        input_grad[:rows],
-        small_sum[3],
-        small_sum[4],
-        jnp.concatenate([attn_grads[0], attn_grads[1], attn_grads[2]], axis=1),
-        attn_grads[3],
-        small_sum[5],
-        small_sum[6],
-        small_sum[:experts].T,
-        jnp.transpose(inner_sum, (1, 0, 2)).astype(wide),
-        jnp.transpose(outer_sum, (1, 0, 2)).astype(wide),
+        finals[0],
+        finals[1],
+        finals[7].reshape(owned),
+        finals[8].reshape(owned),
+        finals[4],
+        finals[5],
+        finals[9].reshape(owned),
+        finals[10].reshape(owned),
+        finals[6].T,
+        jnp.transpose(finals[3], (1, 0, 2)),
+        jnp.transpose(finals[2], (1, 0, 2)),
     )
 
 

time: 260 us -> 216 us (0.83)
  Pallas kernels: 234 us -> 205 us
  other arithmetic: 16.6 us -> 3.38 us
    pallas_call x1, Pallas kernels: 234 us -> 201 us  [grouped(): pl.pallas_call(mega, out_shape=(token_shape, token_shape, jax.ShapeDtypeS...]
    convert_element_type x6 -> x0, other arithmetic: 9.82 us -> none  [the longest x1 3.6 us: grouped(): inner = jnp.transpose(w_in, (1, 0, 2)).astype(low)]
    unnamed x8 -> x12, local copies, waits for them, and re-layouts: 0.02 us -> 6.65 us
    slice x3 -> x0, local copies, waits for them, and re-layouts: 4.23 us -> none  [the longest x1 1.7 us: grouped(): output[:rows]]
    pallas_call x0 -> x1, Pallas kernels: none -> 3.75 us  [grouped(): pl.pallas_call(finish, grid=(experts,), out_shape=(jax.ShapeDtypeStruct((...]
    concatenate x2 -> x0, other arithmetic: 2.69 us -> none  [the longest x1 1.72 us: grouped(): message = jnp.concatenate([cotangent, table], axis=0)]
where the time goes in v3:
time: 216 us
  Pallas kernels  205 us (95%)
  local copies, waits for them, and re-layouts  6.65 us (3%)
  other arithmetic  3.38 us (2%)
    pallas_call x1, Pallas kernels, grouped(): pl.pallas_call(mega, out_shape=(token_shape, token_shape, jax.ShapeDtypeS...  201 us
    unnamed x12, local copies, waits for them, and re-layouts  6.65 us

profile of v3, /device:TPU:0, one launch (start us, length us, event | category | flops | bytes accessed | tf_op | source)
XLA Modules:
  0.0 215.7 jit_solution(5324008943523428416)
XLA Ops:
  0.6 3.4 %convert_bitcast_fusion.outer_ref = bf16[3,384,768]{2,1,0:T(8,128)(2,1)} fusion(f32[384,3,768]{2,0,1:T(8,128)} %param.27), kind=kLoop, calls=%fused_computation | loop fusion | flops 884736 | bytes 5308416 | tf_op jit(solution)/shard_map/convert_element_type | solution.py:1132
  4.0 201.1 %shard_map.221 = (bf16[208,768]{1,0:T(8,128)(2,1)}, bf16[208,768]{1,0:T(8,128)(2,1)}, bf16[3,384,768]{2,1,0:T(8,128)(2,1)}, bf16[3,96,3072]{2,1,0:T(8,128)(2,1)}...) custom-call(bf16[197,768]{1,0:T(8,128)(2,1)} %tok_ref.1, bf16[197,768]{1,0:T(8,128)(2,1)} %cot_ref.1, s32[2,197]{1,0:T(2,128)} %bitcast.19, ...), custom_call_target="tpu_custom_call" | custom-call | tf_op jit(solution)/shard_map/pallas_call | solution.py:1190
  205.1 0.0 copy-start
  205.1 1.5 copy-done
  206.6 0.0 copy-start.1
  206.6 1.5 copy-done.1
  208.1 0.0 copy-start.2
  208.1 1.1 copy-done.2
  209.2 0.0 copy-start.3
  209.2 1.0 copy-done.3
  210.1 0.0 copy-start.4
  210.1 1.0 copy-done.4
  211.1 0.0 copy-start.5
  211.1 0.7 copy-done.5
  211.8 3.8 %shard_map.222 = (bf16[197,768]{1,0:T(8,128)(2,1)}, bf16[197,768]{1,0:T(8,128)(2,1)}, f32[3,384,768]{2,1,0:T(8,128)}, f32[3,96,3072]{2,1,0:T(8,128)}, f32[96,230...) custom-call(bf16[208,768]{1,0:T(8,128)(2,1)S(1)} %copy-done.3, ...), custom_call_target="tpu_custom_call" | custom-call | tf_op jit(solution)/shard_map/pallas_call | solution.py:1229
Async XLA Ops:
  205.1 1.5 copy-start
  206.6 1.5 copy-start.1
  208.1 1.1 copy-start.2
  209.2 1.0 copy-start.3
  210.1 1.0 copy-start.4
  211.1 0.7 copy-start.5

commit v4 on v3

--- a/solution.py
+++ b/solution.py
@@ -251,8 +251,8 @@
 TILE_ROWS = 256
 SENT_ROWS = 208
 CUTS = 4
-Z_STEP = 3.2
-Z_LAG = 1.5
+Z_STEP = 2.4
+Z_LAG = 0.5
 DEPTH = 3
 PIECE = 96
 NEGATIVE = -1e30
@@ -272,7 +272,7 @@
     qkv_ref,
     proj_ref,
     inner_hbm,
-    outer_ref,
+    outer_hbm,
     out_ref,
     igrad_ref,
     go_hbm,
@@ -280,6 +280,7 @@
     ga_hbm,
     piece_ref,
     stage,
+    outer_ref,
     piece,
     table_buf,
     smalls,
@@ -451,6 +452,19 @@
     own_rows = pl.ds(off(shard, PIECE), PIECE)
     small_copies = []
     staged = local(inner_hbm.at[0], stage)
+    tall, wide_cut = outer_ref.shape[1] // 2, 256
+
+    def outer_stage(e):
+        return [
+            local(
+                outer_hbm.at[e, pl.ds(h * tall, tall), pl.ds(c * wide_cut, wide_cut)],
+                probs.at[(e % 2) * 6 + h * 3 + c, pl.ds(0, tall)],
+            )
+            for h in range(2)
+            for c in range(3)
+        ]
+
+    outer_staged = [outer_stage(0), outer_stage(1)]
     experts = router_ref.shape[0]
     piece[...] = jnp.zeros(piece.shape, wide)
     piece[0:experts, 0:PIECE] = router_ref[...]
@@ -495,6 +509,15 @@
         inner_cast(e)
         if e < experts - 1:
             staged = local(inner_hbm.at[e + 1], stage)
+        for copy in outer_staged[e]:
+            copy.wait()
+        for h in range(2):
+            for c in range(3):
+                outer_ref[e, h * tall : (h + 1) * tall, c * wide_cut : (c + 1) * wide_cut] = probs[
+                    (e % 2) * 6 + h * 3 + c, 0:tall, :
+                ].astype(low)
+        if e == 0:
+            outer_staged.append(outer_stage(2))
     gather_q.pass_on()
     half_at = (rep % 2) * (PIECE // 2)
 
@@ -657,11 +680,11 @@
     for g in range(1, 3):
         gather_l.from_s[g].wait_recv()
         lax.fori_loop(2 * g, 2 * g + 2, dispatch_step, 0)
+    gather_u.pass_on()
     inner_own.wait()
     for copy in inner_passed:
         copy.wait_recv()
     hidden_step(0)
-    gather_u.pass_on()
     hidden_step(1)
     hidden_step(2)
     gather_l.from_s[3].wait_recv()
@@ -759,12 +782,11 @@
     plan.sort(key=lambda step: step[:2])
 
     def tend(until):
-        steps = []
         while plan and plan[0][0] <= until:
-            steps.append(plan.pop(0))
-        for _, kind, copies in steps:
-            if kind == 0:
-                assert len(raised) > len(left)
+            _, kind, copies = plan[0]
+            if kind == 0 and len(ready) <= len(left):
+                break
+            plan.pop(0)
 
             @pl.when(is_mid)
             def _():
@@ -1025,28 +1047,28 @@
         ).astype(low)
         swap = send(small_grad.at[step + 1], small_swap.at[step + 1], 2 << step)
         tend(60 + 3 * step)
+    out_sends = [
+        send(sr_out.at[pl.ds(i * SENT_ROWS, SENT_ROWS)], rr_out.at[i - 1], 2 * i)
+        for i in range(1, 4)
+    ]
     tend(72)
     total_share(3, come_p)
     total_share(2, come_v)
     tend(76)
     total_share(1, come_k)
     total_share(0, come_q)
-    out_sends = [
-        send(sr_out.at[pl.ds(i * SENT_ROWS, SENT_ROWS)], rr_out.at[i - 1], 2 * i)
-        for i in range(1, 4)
-    ]
     swap.wait_recv()
     grad_attn[4 * PIECE : 4 * PIECE + 16, :] = (
         small_grad[2].astype(wide) + small_swap[2].astype(wide)
     ).astype(low)
     attn_copies[4].rise()
     tend(84)
+    tend(1000)
     output = resid[0:SENT_ROWS, :] + sr_out[0:SENT_ROWS, :].astype(wide)
     for i in range(3):
         out_sends[i].wait_recv()
         output = output + rr_out[i].astype(wide)
     out_ref[...] = output.astype(low)
-    tend(1000)
     for copies in all_copies:
 
         @pl.when(is_end)
@@ -1129,7 +1151,6 @@
     owned, experts, hidden = w_in.shape
     part = w_out.shape[0]
     shard = lax.axis_index("shard")
-    outer = jnp.transpose(w_out, (1, 0, 2)).astype(low)
     slots = experts * CAP
     total_slots = 8 * slots
     vmem = pltpu.VMEM
@@ -1137,6 +1158,7 @@
     attn_rows = 4 * PIECE + 16
     scratch = [
         vmem((owned, hidden), wide),
+        vmem((experts, part, width), low),
         vmem((16, 128), wide),
         vmem((16, width), wide),
         vmem((8, 16, width), low),
@@ -1183,7 +1205,7 @@
         vmem((3, 16, width), low),
         pltpu.SemaphoreType.DMA((256,)),
         pltpu.SemaphoreType.DMA((256,)),
-        pltpu.SemaphoreType.DMA((48,)),
+        pltpu.SemaphoreType.DMA((64,)),
     ]
     inside = pl.BlockSpec(memory_space=vmem)
     outside = pl.BlockSpec(memory_space=pl.ANY)
@@ -1197,7 +1219,7 @@
             jax.ShapeDtypeStruct((attn_rows, width), low),
             jax.ShapeDtypeStruct((16, 128), wide),
         ),
-        in_specs=[inside] * 12 + [outside, inside],
+        in_specs=[inside] * 12 + [outside, outside],
         out_specs=(inside, inside, outside, outside, outside, inside),
         scratch_shapes=scratch,
         compiler_params=pltpu.CompilerParams(
@@ -1217,7 +1239,7 @@
         w_qkv,
         w_proj,
         jnp.transpose(w_in, (1, 0, 2)),
-        outer,
+        jnp.transpose(w_out, (1, 0, 2)),
     )
 
     def whole(*shape):
@@ -1257,7 +1279,7 @@
             whole(experts, owned),
         )
         + (whole(1, owned),) * 4,
-        compiler_params=pltpu.CompilerParams(vmem_limit_bytes=VMEM_BYTES // 2),
+        compiler_params=pltpu.CompilerParams(vmem_limit_bytes=VMEM_BYTES),
     )(output, input_grad, outer_sum, inner_sum, attn_sum, small_sum)
     return (
         finals[0],

time: 216 us -> 201 us (0.931)
  local copies, waits for them, and re-layouts: 6.65 us -> 0 us
  Pallas kernels: 205 us -> 200 us
  other arithmetic: 3.38 us -> 0 us
    pallas_call x1, Pallas kernels: 201 us -> 194 us  [grouped(): pl.pallas_call(mega, out_shape=(token_shape, token_shape, jax.ShapeDtypeS...]
    unnamed x12 -> x0, local copies, waits for them, and re-layouts: 6.65 us -> none
    convert_element_type x1 -> x0, other arithmetic: 3.38 us -> none  [grouped(): outer = jnp.transpose(w_out, (1, 0, 2)).astype(low)]
    pallas_call x1, Pallas kernels: 3.75 us -> 6.3 us  [grouped(): pl.pallas_call(finish, grid=(experts,), out_shape=(jax.ShapeDtypeStruct((...]
where the time goes in v4:
time: 201 us
  Pallas kernels  200 us (100%)
    pallas_call x1, Pallas kernels, grouped(): pl.pallas_call(mega, out_shape=(token_shape, token_shape, jax.ShapeDtypeS...  194 us
    pallas_call x1, Pallas kernels, grouped(): pl.pallas_call(finish, grid=(experts,), out_shape=(jax.ShapeDtypeStruct((...  6.3 us

profile of v4, /device:TPU:0, one launch (start us, length us, event | category | flops | bytes accessed | tf_op | source)
XLA Modules:
  0.0 200.8 jit_solution(15713326065509476794)
XLA Ops:
  0.6 193.6 %shard_map.221 = (bf16[208,768]{1,0:T(8,128)(2,1)}, bf16[208,768]{1,0:T(8,128)(2,1)}, bf16[3,384,768]{2,1,0:T(8,128)(2,1)}, bf16[3,96,3072]{2,1,0:T(8,128)(2,1)}...) custom-call(bf16[197,768]{1,0:T(8,128)(2,1)} %tok_ref.1, bf16[197,768]{1,0:T(8,128)(2,1)} %cot_ref.1, s32[2,197]{1,0:T(2,128)} %bitcast.19, ...), custom_call_target="tpu_custom_call" | custom-call | tf_op jit(solution)/shard_map/pallas_call | solution.py:1212
  194.3 6.3 %shard_map.222 = (bf16[197,768]{1,0:T(8,128)(2,1)}, bf16[197,768]{1,0:T(8,128)(2,1)}, f32[3,384,768]{2,1,0:T(8,128)}, f32[3,96,3072]{2,1,0:T(8,128)}, f32[96,230...) custom-call(bf16[208,768]{1,0:T(8,128)(2,1)} %get-tuple-element.28.o, ...), custom_call_target="tpu_custom_call" | custom-call | tf_op jit(solution)/shard_map/pallas_call | solution.py:1251

commit v5 on v4

--- a/solution.py
+++ b/solution.py
@@ -605,7 +605,7 @@
         heads[:, head_columns(p, 0)] = jnp.where(lane < 64, mixed[0], mixed[1]).astype(low)
         return carry
 
-    lax.fori_loop(0, 6, attend, 0)
+    lax.fori_loop(0, 6, attend, 0, unroll=2)
     gather_p.last()
     for copy in gather_p.from_s:
         copy.wait_recv()
@@ -669,7 +669,7 @@
             ).astype(low)
             return carry
 
-        lax.fori_loop(0, experts, step, 0)
+        lax.fori_loop(0, experts, step, 0, unroll=True)
 
     gather_l.pass_on()
     gather_u = Gather(row_view(ups_base), (0, 112), (112, 96))
@@ -693,7 +693,7 @@
     hidden_step(3)
     for copy in gather_u.from_s:
         copy.wait_recv()
-    lax.fori_loop(0, 8, upward_step, 0)
+    lax.fori_loop(0, 8, upward_step, 0, unroll=2)
 
     ready, raised, left = [], [], []
 
@@ -866,7 +866,7 @@
             grad_in_send(e)
         tend(4 + 2 * e)
     for e in range(experts):
-        lax.fori_loop(2 * e, 2 * e + 2, back_step, 0)
+        lax.fori_loop(2 * e, 2 * e + 2, back_step, 0, unroll=True)
         tend(10.5 + 2.3 * e)
 
     def combine_back(j):
@@ -999,9 +999,9 @@
     work[3 * width : 4 * width, :] = contract(heads[...], agrad[...], 0, 0).astype(low)
     share_p = share(3)
     tend(43)
-    lax.fori_loop(0, 3, attend_back, 0)
+    lax.fori_loop(0, 3, attend_back, 0, unroll=True)
     tend(46)
-    lax.fori_loop(3, 6, attend_back, 0)
+    lax.fori_loop(3, 6, attend_back, 0, unroll=True)
     tend(50)
 
     def weight_grad_of(part):
@@ -1047,16 +1047,16 @@
         ).astype(low)
         swap = send(small_grad.at[step + 1], small_swap.at[step + 1], 2 << step)
         tend(60 + 3 * step)
-    out_sends = [
-        send(sr_out.at[pl.ds(i * SENT_ROWS, SENT_ROWS)], rr_out.at[i - 1], 2 * i)
-        for i in range(1, 4)
-    ]
     tend(72)
     total_share(3, come_p)
     total_share(2, come_v)
     tend(76)
     total_share(1, come_k)
     total_share(0, come_q)
+    out_sends = [
+        send(sr_out.at[pl.ds(i * SENT_ROWS, SENT_ROWS)], rr_out.at[i - 1], 2 * i)
+        for i in range(1, 4)
+    ]
     swap.wait_recv()
     grad_attn[4 * PIECE : 4 * PIECE + 16, :] = (
         small_grad[2].astype(wide) + small_swap[2].astype(wide)

time: 201 us -> 200 us (level)
  no operation moved by 1% of the time
where the time goes in v5:
time: 200 us
  Pallas kernels  199 us (100%)
    pallas_call x1, Pallas kernels, grouped(): pl.pallas_call(mega, out_shape=(token_shape, token_shape, jax.ShapeDtypeS...  193 us
    pallas_call x1, Pallas kernels, grouped(): pl.pallas_call(finish, grid=(experts,), out_shape=(jax.ShapeDtypeStruct((...  6.3 us

profile of v5, /device:TPU:0, one launch (start us, length us, event | category | flops | bytes accessed | tf_op | source)
XLA Modules:
  0.0 199.7 jit_solution(14232848727836851395)
XLA Ops:
  0.6 192.6 %shard_map.221 = (bf16[208,768]{1,0:T(8,128)(2,1)}, bf16[208,768]{1,0:T(8,128)(2,1)}, bf16[3,384,768]{2,1,0:T(8,128)(2,1)}, bf16[3,96,3072]{2,1,0:T(8,128)(2,1)}...) custom-call(bf16[197,768]{1,0:T(8,128)(2,1)} %tok_ref.1, bf16[197,768]{1,0:T(8,128)(2,1)} %cot_ref.1, s32[2,197]{1,0:T(2,128)} %bitcast.19, ...), custom_call_target="tpu_custom_call" | custom-call | tf_op jit(solution)/shard_map/pallas_call | solution.py:1212
  193.2 6.3 %shard_map.222 = (bf16[197,768]{1,0:T(8,128)(2,1)}, bf16[197,768]{1,0:T(8,128)(2,1)}, f32[3,384,768]{2,1,0:T(8,128)}, f32[3,96,3072]{2,1,0:T(8,128)}, f32[96,230...) custom-call(bf16[208,768]{1,0:T(8,128)(2,1)} %get-tuple-element.28.o, ...), custom_call_target="tpu_custom_call" | custom-call | tf_op jit(solution)/shard_map/pallas_call | solution.py:1251
